TPU v7x, 32 devices: a whole 2x2x4 slice. The times are simulated.
32 devices in a mesh: dp: 8 (over y, x, core), seq: 4 (over z).
Axes of the slice: x: 2, y: 2, z: 4, core: 2. Of those that a mesh axis runs over, the one named last changes fastest.
Arguments:
- acoustic_features: bfloat16 [64, 512, 768], P('dp', 'seq'), may hold values from -6 to 6
- upstream_derivative: bfloat16 [64, 512, 768], P('dp', 'seq'), may hold values from -6 to 6
- flat_random_draws: float32 [64, 512, 200], P('dp', 'seq'), may hold values from 0.02 to 0.98
- softening_scalar: float32 [1], replicated, may hold values from 0.5 to 2
- valid_frame_counts: int32 [64], P('dp'), may hold values from 256 to 512, as said below
- hidden_run_beginnings: int32 [64, 36], P('dp'), may hold values from 0 to 511
- hidden_run_sizes: int32 [64, 36], P('dp'), may hold values from 1 to 20
- distance_bins: int32 [1023], replicated, may hold values from 0 to 319
- hidden_frame_vector: bfloat16 [768], P(('dp', 'seq')), may hold values from -6 to 6
- premix_scale_vector: bfloat16 [768], P(('dp', 'seq')), may hold values from 0.5 to 1.5
- premix_shift_vector: bfloat16 [768], P(('dp', 'seq')), may hold values from -1.25 to 1.25
- question_map: bfloat16 [768, 768], P(('dp', 'seq')), may hold values from -0.21875 to 0.21875
- question_shift: bfloat16 [768], P(('dp', 'seq')), may hold values from -1.25 to 1.25
- lookup_address_map: bfloat16 [768, 768], P(('dp', 'seq')), may hold values from -0.21875 to 0.21875
- content_map: bfloat16 [768, 768], P(('dp', 'seq')), may hold values from -0.21875 to 0.21875
- content_shift: bfloat16 [768], P(('dp', 'seq')), may hold values from -1.25 to 1.25
- mixing_result_map: bfloat16 [768, 768], P(('dp', 'seq')), may hold values from -0.875 to 0.875
- mixing_result_shift: bfloat16 [768], P(('dp', 'seq')), may hold values from -1.25 to 1.25
- distance_bin_shifts: bfloat16 [3840], P(('dp', 'seq')), may hold values from -6 to 6
- premlp_scale_vector: bfloat16 [768], P(('dp', 'seq')), may hold values from 0.5 to 1.5
- premlp_shift_vector: bfloat16 [768], P(('dp', 'seq')), may hold values from -1.25 to 1.25
- perceptron_entry_map: bfloat16 [768, 3072], P(('dp', 'seq')), may hold values from -0.21875 to 0.21875
- perceptron_inner_shift: bfloat16 [3072], P(('dp', 'seq')), may hold values from -1.25 to 1.25
- perceptron_final_map: bfloat16 [3072, 768], P(('dp', 'seq')), may hold values from -0.109375 to 0.109375
- perceptron_final_shift: bfloat16 [768], P(('dp', 'seq')), may hold values from -1.25 to 1.25
- codeword_score_map: bfloat16 [768, 200], P(('dp', 'seq')), may hold values from -0.21875 to 0.21875
- codeword_vectors: bfloat16 [25600], P(('dp', 'seq')), may hold values from -6 to 6
- contrast_space_map: bfloat16 [768, 256], P(('dp', 'seq')), may hold values from -0.21875 to 0.21875
- contrast_space_shift: bfloat16 [256], P(('dp', 'seq')), may hold values from -1.25 to 1.25
Outputs:
- encoded: bfloat16 [64, 512, 768], P('dp', 'seq')
- frames_grad: float32 [64, 512, 768], P('dp', 'seq')
- mask_vector_grad: float32 [768], P(('dp', 'seq'))
- attn_gain_grad: float32 [768], P(('dp', 'seq'))
- attn_shift_grad: float32 [768], P(('dp', 'seq'))
- query_weight_grad: float32 [768, 768], P(('dp', 'seq'))
- query_bias_grad: float32 [768], P(('dp', 'seq'))
- key_weight_grad: float32 [768, 768], P(('dp', 'seq'))
- value_weight_grad: float32 [768, 768], P(('dp', 'seq'))
- value_bias_grad: float32 [768], P(('dp', 'seq'))
- output_weight_grad: float32 [768, 768], P(('dp', 'seq'))
- output_bias_grad: float32 [768], P(('dp', 'seq'))
- position_table_grad: float32 [3840], P(('dp', 'seq'))
- ffn_gain_grad: float32 [768], P(('dp', 'seq'))
- ffn_shift_grad: float32 [768], P(('dp', 'seq'))
- inner_weight_grad: float32 [768, 3072], P(('dp', 'seq'))
- inner_bias_grad: float32 [3072], P(('dp', 'seq'))
- outer_weight_grad: float32 [3072, 768], P(('dp', 'seq'))
- outer_bias_grad: float32 [768], P(('dp', 'seq'))
- quant_weight_grad: float32 [768, 200], P(('dp', 'seq'))
- codebook_grad: float32 [25600], P(('dp', 'seq'))
- proj_weight_grad: float32 [768, 256], P(('dp', 'seq'))
- proj_bias_grad: float32 [256], P(('dp', 'seq'))
Inputs may be any that keep to these rules, and one draw needn't show every extreme that they name: `valid_frame_counts`: in each aligned block of 8 utterances (those of one index of dp) at least one has all 512 frames valid.
All inputs are finite; a program needn't handle non-finite values.
Results may differ from a plain program's by a relative error of at most 0.014.
Values may be sent and summed in bfloat16 or wider, within the bound.
No kernel may reach another device: no remote copies, remote signals or barrier semaphores. Data moves between devices by JAX's collectives and lax.ppermute only.
A program may use at most 256 MiB of HBM per device.

v0:
```python
import math

import jax
import jax.numpy as jnp
from jax import lax
from jax.sharding import PartitionSpec as P

D = 768
H = 12
HD = 64
NB = 320
CODE_GROUPS = 2
GROUP_CODES = 100
CDG = 128
UTT_FRAMES = 512


EPSILON = 1e-05
CONTRAST_SCALE = 0.05
NEGATIVE = -1000000000.0
HIGHEST = lax.Precision.HIGHEST


def layer_norm(values, norm_gain, norm_shift):
    row_mean = jnp.mean(values, axis=-1, keepdims=True)
    centred = values - row_mean
    variance = jnp.mean(centred * centred, axis=-1, keepdims=True)
    return centred * lax.rsqrt(variance + EPSILON) * norm_gain + norm_shift


def normalize(values):
    return values * lax.rsqrt(jnp.sum(values * values, axis=-1, keepdims=True) + EPSILON)


def softmax_last(scores):
    row_max = jnp.max(scores, axis=-1, keepdims=True)
    exp_terms = jnp.exp(scores - row_max)
    return exp_terms / jnp.sum(exp_terms, axis=-1, keepdims=True)


def gelu_exact(values):
    return jax.nn.gelu(values, approximate=False)


def codeword_chances(codeword_scores, extreme_noise, softening_factor):
    softened_scores = ((codeword_scores + extreme_noise) / softening_factor).reshape(
        codeword_scores.shape[0], CODE_GROUPS, GROUP_CODES
    )
    return softmax_last(softened_scores)


def project(left_side, right_side):
    return jnp.dot(left_side, right_side, preferred_element_type=jnp.float32)


def project_back(left_side, right_side):
    return lax.dot_general(
        left_side, right_side, (((1,), (1,)), ((), ())), preferred_element_type=jnp.float32
    )


def weight_grad(left_side, right_side):
    return lax.dot_general(
        left_side, right_side, (((0,), (0,)), ((), ())), preferred_element_type=jnp.float32
    )


def row_total(values):
    return jnp.sum(values.astype(jnp.float32), axis=0)


def body(
    acoustic_features,
    upstream_derivative,
    flat_random_draws,
    softening_scalar,
    valid_frame_counts,
    hidden_run_beginnings,
    hidden_run_sizes,
    distance_bins,
    hidden_frame_vector,
    premix_scale_vector,
    premix_shift_vector,
    question_map,
    question_shift,
    lookup_address_map,
    content_map,
    content_shift,
    mixing_result_map,
    mixing_result_shift,
    distance_bin_shifts,
    premlp_scale_vector,
    premlp_shift_vector,
    perceptron_entry_map,
    perceptron_inner_shift,
    perceptron_final_map,
    perceptron_final_shift,
    codeword_score_map,
    codeword_vectors,
    contrast_space_map,
    contrast_space_shift,
):
    frames_in, cotangent_in, gumbel_in = (acoustic_features, upstream_derivative, flat_random_draws)
    my_lengths, my_starts, my_spans = (valid_frame_counts, hidden_run_beginnings, hidden_run_sizes)
    first_frame = lax.axis_index("seq") * acoustic_features.shape[1]
    utterances = frames_in.shape[0]
    frame_count = frames_in.shape[1]
    row_count = utterances * frame_count
    head_pairs = H // 2
    score_scale = 1.0 / math.sqrt(HD)
    position = first_frame + jnp.arange(frame_count, dtype=jnp.int32)
    all_frames = jnp.arange(UTT_FRAMES, dtype=jnp.int32)
    span_ends = my_starts + my_spans
    covered = jnp.any(
        (my_starts[:, :, None] <= all_frames[None, None, :])
        & (all_frames[None, None, :] < span_ends[:, :, None]),
        axis=1,
    )
    key_valid = all_frames[None, :] < my_lengths[:, None]
    masked_all = covered & key_valid
    masked_here = lax.dynamic_slice_in_dim(masked_all, first_frame, frame_count, 1)
    mask_rows = masked_here.reshape(row_count, 1)

    def attention_weights():
        return (
            lax.all_gather(hidden_frame_vector, ("dp", "seq"), axis=0, tiled=True),
            lax.all_gather(premix_scale_vector, ("dp", "seq"), axis=0, tiled=True),
            lax.all_gather(premix_shift_vector, ("dp", "seq"), axis=0, tiled=True),
            lax.all_gather(question_map, ("dp", "seq"), axis=0, tiled=True),
            lax.all_gather(question_shift, ("dp", "seq"), axis=0, tiled=True),
            lax.all_gather(lookup_address_map, ("dp", "seq"), axis=0, tiled=True),
            lax.all_gather(content_map, ("dp", "seq"), axis=0, tiled=True),
            lax.all_gather(content_shift, ("dp", "seq"), axis=0, tiled=True),
            lax.all_gather(mixing_result_map, ("dp", "seq"), axis=0, tiled=True),
            lax.all_gather(mixing_result_shift, ("dp", "seq"), axis=0, tiled=True),
            lax.all_gather(distance_bin_shifts, ("dp", "seq"), axis=0, tiled=True),
        )

    def feedforward_weights():
        return (
            lax.all_gather(premlp_scale_vector, ("dp", "seq"), axis=0, tiled=True),
            lax.all_gather(premlp_shift_vector, ("dp", "seq"), axis=0, tiled=True),
            lax.all_gather(perceptron_entry_map, ("dp", "seq"), axis=0, tiled=True),
            lax.all_gather(perceptron_inner_shift, ("dp", "seq"), axis=0, tiled=True),
            lax.all_gather(perceptron_final_map, ("dp", "seq"), axis=0, tiled=True),
            lax.all_gather(perceptron_final_shift, ("dp", "seq"), axis=0, tiled=True),
        )

    def head_weights():
        return (
            lax.all_gather(codeword_score_map, ("dp", "seq"), axis=0, tiled=True),
            lax.all_gather(codeword_vectors, ("dp", "seq"), axis=0, tiled=True),
            lax.all_gather(contrast_space_map, ("dp", "seq"), axis=0, tiled=True),
            lax.all_gather(contrast_space_shift, ("dp", "seq"), axis=0, tiled=True),
        )

    attn_full = attention_weights()
    frame_rows = frames_in.reshape(row_count, D)
    start_rows = jnp.where(
        mask_rows, attn_full[0].astype(jnp.float32)[None, :], frame_rows.astype(jnp.float32)
    )
    normed_attn, attn_norm_back = jax.vjp(
        layer_norm, start_rows, attn_full[1].astype(jnp.float32), attn_full[2].astype(jnp.float32)
    )
    normed_low = normed_attn.astype(jnp.bfloat16)
    queries = (project(normed_low, attn_full[3]) + attn_full[4].astype(jnp.float32)).astype(
        jnp.bfloat16
    )
    keys_here = (
        project(normed_low, attn_full[5]).astype(jnp.bfloat16).reshape(utterances, frame_count, D)
    )
    values_here = (
        (project(normed_low, attn_full[6]) + attn_full[7].astype(jnp.float32))
        .astype(jnp.bfloat16)
        .reshape(utterances, frame_count, D)
    )
    keys_all, values_all = (
        lax.all_gather(keys_here, "seq", axis=1, tiled=True),
        lax.all_gather(values_here, "seq", axis=1, tiled=True),
    )
    bucket_hits = (distance_bins[:, None] == jnp.arange(NB, dtype=jnp.int32)[None, :]).astype(
        jnp.float32
    )
    offsets = all_frames[None, :] - position[:, None] + (UTT_FRAMES - 1)

    def local_bias(table_flat):
        per_offset = lax.dot_general(
            table_flat.reshape(H, NB),
            bucket_hits,
            (((1,), (1,)), ((), ())),
            precision=HIGHEST,
            preferred_element_type=jnp.float32,
        )
        return per_offset[:, offsets]

    distance_shift, bias_back = jax.vjp(local_bias, attn_full[10].astype(jnp.float32))
    query_heads = queries.reshape(utterances, frame_count, head_pairs, 2, HD)
    key_heads = keys_all.reshape(utterances, UTT_FRAMES, head_pairs, 2, HD)
    value_heads = values_all.reshape(utterances, UTT_FRAMES, head_pairs, 2, HD)
    bias_pairs = distance_shift.reshape(head_pairs, 2, frame_count, UTT_FRAMES)

    def pair_slices(pair_index):
        return (
            lax.dynamic_index_in_dim(query_heads, pair_index, 2, keepdims=False),
            lax.dynamic_index_in_dim(key_heads, pair_index, 2, keepdims=False),
            lax.dynamic_index_in_dim(value_heads, pair_index, 2, keepdims=False),
            lax.dynamic_index_in_dim(bias_pairs, pair_index, 0, keepdims=False),
        )

    def pair_scores(query_pair, key_pair, bias_pair):
        product = jnp.einsum(
            "uihe,ujhe->uhij", query_pair, key_pair, preferred_element_type=jnp.float32
        )
        return jnp.where(
            key_valid[:, None, None, :], product * score_scale + bias_pair[None], NEGATIVE
        )

    def attend(pair_index):
        query_pair, key_pair, value_pair, bias_pair = pair_slices(pair_index)
        scores = pair_scores(query_pair, key_pair, bias_pair)
        row_max = jnp.max(scores, axis=-1, keepdims=True)
        exp_terms = jnp.exp(scores - row_max)
        sum_terms = jnp.sum(exp_terms, axis=-1, keepdims=True)
        attn_probs = (exp_terms / sum_terms).astype(jnp.bfloat16)
        mixed_pair = jnp.einsum(
            "uhij,ujhe->uihe", attn_probs, value_pair, preferred_element_type=jnp.float32
        )
        return (mixed_pair, row_max + jnp.log(sum_terms))

    mixed_pairs, log_totals = lax.map(attend, jnp.arange(head_pairs))
    mixed_low = jnp.moveaxis(mixed_pairs, 0, 2).reshape(row_count, D).astype(jnp.bfloat16)
    middle = start_rows + project(mixed_low, attn_full[8]) + attn_full[9].astype(jnp.float32)
    ffn_full = feedforward_weights()
    normed_ffn, ffn_norm_back = jax.vjp(
        layer_norm, middle, ffn_full[0].astype(jnp.float32), ffn_full[1].astype(jnp.float32)
    )
    normed_ffn_low = normed_ffn.astype(jnp.bfloat16)
    inner_act = project(normed_ffn_low, ffn_full[2]) + ffn_full[3].astype(jnp.float32)
    activated, gelu_back = jax.vjp(gelu_exact, inner_act)
    activated_low = activated.astype(jnp.bfloat16)
    encoded = middle + project(activated_low, ffn_full[4]) + ffn_full[5].astype(jnp.float32)
    encoded_low = encoded.astype(jnp.bfloat16)
    head_full = head_weights()
    projected = project(encoded_low, head_full[2]) + head_full[3].astype(jnp.float32)
    unit_pred, pred_back = jax.vjp(normalize, projected)
    pred_blocks = unit_pred.astype(jnp.bfloat16).reshape(utterances, frame_count, CODE_GROUPS * CDG)
    extreme_noise = -jnp.log(-jnp.log(gumbel_in.reshape(row_count, CODE_GROUPS * GROUP_CODES)))
    softening_factor = softening_scalar[0]
    codeword_scores = project(frame_rows, head_full[0])
    code_probs, code_back = jax.vjp(
        lambda incoming_scores: codeword_chances(incoming_scores, extreme_noise, softening_factor),
        codeword_scores,
    )
    code_low = code_probs.astype(jnp.bfloat16)
    target_raw = jnp.einsum(
        "rgv,gvc->rgc",
        code_low,
        head_full[1].reshape(CODE_GROUPS, GROUP_CODES, CDG),
        preferred_element_type=jnp.float32,
    ).reshape(row_count, CODE_GROUPS * CDG)
    target_unit, target_back = jax.vjp(normalize, target_raw)
    target_here = target_unit.astype(jnp.bfloat16).reshape(
        utterances, frame_count, CODE_GROUPS * CDG
    )
    targets_all = lax.all_gather(target_here, "seq", axis=1, tiled=True)
    similarity = jnp.einsum(
        "uie,uje->uij", pred_blocks, targets_all, preferred_element_type=jnp.float32
    )
    logits = jnp.where(masked_all[:, None, :], similarity / CONTRAST_SCALE, NEGATIVE)
    soft_probs = softmax_last(logits)
    own_hits = (all_frames[None, :] == position[:, None]).astype(jnp.float32)
    logit_grad = jnp.where(masked_here[:, :, None], soft_probs - own_hits[None], 0.0)
    logit_low = (logit_grad / CONTRAST_SCALE).astype(jnp.bfloat16)
    pred_grad = jnp.einsum(
        "uij,uje->uie", logit_low, targets_all, preferred_element_type=jnp.float32
    ).reshape(row_count, CODE_GROUPS * CDG)
    target_terms = jnp.einsum(
        "uij,uie->uje", logit_low, pred_blocks, preferred_element_type=jnp.float32
    )
    unit_grad = (
        lax.psum_scatter(target_terms.astype(jnp.bfloat16), "seq", scatter_dimension=1, tiled=True)
        .astype(jnp.float32)
        .reshape(row_count, CODE_GROUPS * CDG)
    )
    head_back = head_weights()
    (target_raw_grad,) = target_back(unit_grad)
    target_low = target_raw_grad.astype(jnp.bfloat16).reshape(row_count, CODE_GROUPS, CDG)
    codebook_grad = jnp.einsum(
        "rgv,rgc->gvc", code_low, target_low, preferred_element_type=jnp.float32
    ).reshape(CODE_GROUPS * GROUP_CODES * CDG)
    probs_grad = jnp.einsum(
        "rgc,gvc->rgv",
        target_low,
        head_back[1].reshape(CODE_GROUPS, GROUP_CODES, CDG),
        preferred_element_type=jnp.float32,
    )
    (logits_grad,) = code_back(probs_grad)
    logits_low = logits_grad.astype(jnp.bfloat16)
    quant_grad = weight_grad(frame_rows, logits_low)
    code_path = project_back(logits_low, head_back[0])
    (projected_grad,) = pred_back(pred_grad)
    projected_low = projected_grad.astype(jnp.bfloat16)
    proj_weight_grad = weight_grad(encoded_low, projected_low)
    proj_bias_grad = row_total(projected_low)
    output_grad = cotangent_in.reshape(row_count, D).astype(jnp.float32) + project_back(
        projected_low, head_back[2]
    )
    ffn_back = feedforward_weights()
    branch_low = output_grad.astype(jnp.bfloat16)
    outer_weight_grad = weight_grad(activated_low, branch_low)
    outer_bias_grad = row_total(branch_low)
    (inner_grad,) = gelu_back(project_back(branch_low, ffn_back[4]))
    inner_low = inner_grad.astype(jnp.bfloat16)
    inner_weight_grad = weight_grad(normed_ffn_low, inner_low)
    inner_bias_grad = row_total(inner_low)
    middle_norm_grad, ffn_gain_grad, ffn_shift_grad = ffn_norm_back(
        project_back(inner_low, ffn_back[2])
    )
    middle_grad = output_grad + middle_norm_grad
    attn_back = attention_weights()
    attn_low = middle_grad.astype(jnp.bfloat16)
    output_weight_grad = weight_grad(mixed_low, attn_low)
    output_bias_grad = row_total(attn_low)
    mixed_grad = (
        project_back(attn_low, attn_back[8])
        .astype(jnp.bfloat16)
        .reshape(utterances, frame_count, head_pairs, 2, HD)
    )

    def attend_back(pair_index):
        query_pair, key_pair, value_pair, bias_pair = pair_slices(pair_index)
        mixed_pair = lax.dynamic_index_in_dim(mixed_grad, pair_index, 2, keepdims=False)
        log_total = lax.dynamic_index_in_dim(log_totals, pair_index, 0, keepdims=False)
        attn_probs = jnp.exp(pair_scores(query_pair, key_pair, bias_pair) - log_total)
        probs_pair = jnp.einsum(
            "uihe,ujhe->uhij", mixed_pair, value_pair, preferred_element_type=jnp.float32
        )
        spread = jnp.sum(attn_probs * probs_pair, axis=-1, keepdims=True)
        score_grad = attn_probs * (probs_pair - spread)
        score_low = (score_grad * score_scale).astype(jnp.bfloat16)
        query_part = jnp.einsum(
            "uhij,ujhe->uihe", score_low, key_pair, preferred_element_type=jnp.float32
        )
        key_part = jnp.einsum(
            "uhij,uihe->ujhe", score_low, query_pair, preferred_element_type=jnp.float32
        )
        value_part = jnp.einsum(
            "uhij,uihe->ujhe",
            attn_probs.astype(jnp.bfloat16),
            mixed_pair,
            preferred_element_type=jnp.float32,
        )
        return (query_part, key_part, value_part, jnp.sum(score_grad, axis=0))

    query_parts, key_parts, value_parts, bias_parts = lax.map(attend_back, jnp.arange(head_pairs))
    query_low = jnp.moveaxis(query_parts, 0, 2).reshape(row_count, D).astype(jnp.bfloat16)
    key_terms = jnp.moveaxis(key_parts, 0, 2).reshape(utterances, UTT_FRAMES, D)
    value_terms = jnp.moveaxis(value_parts, 0, 2).reshape(utterances, UTT_FRAMES, D)
    key_sum, value_sum = (
        lax.psum_scatter(
            key_terms.astype(jnp.bfloat16), "seq", scatter_dimension=1, tiled=True
        ).astype(jnp.float32),
        lax.psum_scatter(
            value_terms.astype(jnp.bfloat16), "seq", scatter_dimension=1, tiled=True
        ).astype(jnp.float32),
    )
    key_low = key_sum.reshape(row_count, D).astype(jnp.bfloat16)
    value_low = value_sum.reshape(row_count, D).astype(jnp.bfloat16)
    query_weight_grad = weight_grad(normed_low, query_low)
    query_bias_grad = row_total(query_low)
    key_weight_grad = weight_grad(normed_low, key_low)
    value_weight_grad = weight_grad(normed_low, value_low)
    value_bias_grad = row_total(value_low)
    normed_grad = (
        project_back(query_low, attn_back[3])
        + project_back(key_low, attn_back[5])
        + project_back(value_low, attn_back[6])
    )
    start_norm_grad, attn_gain_grad, attn_shift_grad = attn_norm_back(normed_grad)
    start_grad = middle_grad + start_norm_grad
    mask_vector_grad = jnp.sum(jnp.where(mask_rows, start_grad, 0.0), axis=0)
    frames_grad = jnp.where(mask_rows, 0.0, start_grad) + code_path
    (table_grad,) = bias_back(bias_parts.reshape(H, frame_count, UTT_FRAMES))
    attn_shards = (
        lax.psum_scatter(mask_vector_grad, ("dp", "seq"), scatter_dimension=0, tiled=True),
        lax.psum_scatter(attn_gain_grad, ("dp", "seq"), scatter_dimension=0, tiled=True),
        lax.psum_scatter(attn_shift_grad, ("dp", "seq"), scatter_dimension=0, tiled=True),
        lax.psum_scatter(query_weight_grad, ("dp", "seq"), scatter_dimension=0, tiled=True),
        lax.psum_scatter(query_bias_grad, ("dp", "seq"), scatter_dimension=0, tiled=True),
        lax.psum_scatter(key_weight_grad, ("dp", "seq"), scatter_dimension=0, tiled=True),
        lax.psum_scatter(value_weight_grad, ("dp", "seq"), scatter_dimension=0, tiled=True),
        lax.psum_scatter(value_bias_grad, ("dp", "seq"), scatter_dimension=0, tiled=True),
        lax.psum_scatter(output_weight_grad, ("dp", "seq"), scatter_dimension=0, tiled=True),
        lax.psum_scatter(output_bias_grad, ("dp", "seq"), scatter_dimension=0, tiled=True),
        lax.psum_scatter(table_grad, ("dp", "seq"), scatter_dimension=0, tiled=True),
    )
    ffn_shards = (
        lax.psum_scatter(ffn_gain_grad, ("dp", "seq"), scatter_dimension=0, tiled=True),
        lax.psum_scatter(ffn_shift_grad, ("dp", "seq"), scatter_dimension=0, tiled=True),
        lax.psum_scatter(inner_weight_grad, ("dp", "seq"), scatter_dimension=0, tiled=True),
        lax.psum_scatter(inner_bias_grad, ("dp", "seq"), scatter_dimension=0, tiled=True),
        lax.psum_scatter(outer_weight_grad, ("dp", "seq"), scatter_dimension=0, tiled=True),
        lax.psum_scatter(outer_bias_grad, ("dp", "seq"), scatter_dimension=0, tiled=True),
    )
    head_shards = (
        lax.psum_scatter(quant_grad, ("dp", "seq"), scatter_dimension=0, tiled=True),
        lax.psum_scatter(codebook_grad, ("dp", "seq"), scatter_dimension=0, tiled=True),
        lax.psum_scatter(proj_weight_grad, ("dp", "seq"), scatter_dimension=0, tiled=True),
        lax.psum_scatter(proj_bias_grad, ("dp", "seq"), scatter_dimension=0, tiled=True),
    )
    encoded_out = encoded_low.reshape(utterances, frame_count, D)
    grad_out = frames_grad.reshape(utterances, frame_count, D)
    return (encoded_out, grad_out) + tuple(attn_shards) + tuple(ffn_shards) + tuple(head_shards)


def solution(mesh):
    placed = (
        P("dp", "seq", None),
        P("dp", "seq", None),
        P("dp", "seq", None),
        P(),
        P("dp"),
        P("dp", None),
        P("dp", None),
        P(),
        P(("dp", "seq")),
        P(("dp", "seq")),
        P(("dp", "seq")),
        P(("dp", "seq"), None),
        P(("dp", "seq")),
        P(("dp", "seq"), None),
        P(("dp", "seq"), None),
        P(("dp", "seq")),
        P(("dp", "seq"), None),
        P(("dp", "seq")),
        P(("dp", "seq")),
        P(("dp", "seq")),
        P(("dp", "seq")),
        P(("dp", "seq"), None),
        P(("dp", "seq")),
        P(("dp", "seq"), None),
        P(("dp", "seq")),
        P(("dp", "seq"), None),
        P(("dp", "seq")),
        P(("dp", "seq"), None),
        P(("dp", "seq")),
    )
    return jax.shard_map(
        body,
        mesh=mesh,
        in_specs=placed,
        out_specs=(
            P("dp", "seq", None),
            P("dp", "seq", None),
            P(("dp", "seq")),
            P(("dp", "seq")),
            P(("dp", "seq")),
            P(("dp", "seq"), None),
            P(("dp", "seq")),
            P(("dp", "seq"), None),
            P(("dp", "seq"), None),
            P(("dp", "seq")),
            P(("dp", "seq"), None),
            P(("dp", "seq")),
            P(("dp", "seq")),
            P(("dp", "seq")),
            P(("dp", "seq")),
            P(("dp", "seq"), None),
            P(("dp", "seq")),
            P(("dp", "seq"), None),
            P(("dp", "seq")),
            P(("dp", "seq"), None),
            P(("dp", "seq")),
            P(("dp", "seq"), None),
            P(("dp", "seq")),
        ),
        check_vma=False,
    )
```

profile of v0, /device:TPU:0, one launch (start us, length us, event | category | flops | bytes accessed | tf_op | source)
XLA Modules:
  0.0 2485.7 jit_solution(14051816431267011248)
XLA Ops:
  23.9 130.0 %all-reduce.33.cloned.1.call-done = (bf16[768]{0:T(1024)(128)(2,1)}, bf16[768]{0:T(1024)(128)(2,1)}, bf16[768]{0:T(1024)(128)(2,1)}, bf16[768]{0:T(1024)(128)(2,...) async-done(((bf16[768]{0:T(1024)(128)(2,1)}, ...) | async-done | bytes 79376
  161.2 52.4 %all-gather.10.cloned.1.call-done = bf16[768,768]{1,0:T(8,128)(2,1)} async-done(((bf16[24,768]{1,0:T(8,128)(2,1)}), bf16[768,768]{1,0:T(8,128)(2,1)}) %all-gather.10.cloned.1.call-update) | async-done | bytes 1179664 | tf_op jit(solution)/shard_map/all_gather | solution.py:132
  220.0 49.4 %all-gather.16.cloned.1.call-done = bf16[768,768]{1,0:T(8,128)(2,1)} async-done(((bf16[24,768]{1,0:T(8,128)(2,1)}), bf16[768,768]{1,0:T(8,128)(2,1)}) %all-gather.16.cloned.1.call-update) | async-done | bytes 1179664 | tf_op jit(solution)/shard_map/all_gather | solution.py:131
  279.1 71.1 %all_gather.102 = bf16[768,200]{1,0:T(8,128)(2,1)S(1)} all-gather(bf16[24,200]{1,0:T(8,128)(2,1)S(1)} %copy-done.81), channel_id=1, replica_groups=mesh['dp'=8,'seq'=4] {'dp','seq'}, dimensions={0}, use_global_device_ids=true | all-gather | bytes 316800 | tf_op jit(solution)/shard_map/all_gather | solution.py:151
  353.2 143.5 %all_gather.100 = bf16[768,256]{1,0:T(8,128)(2,1)} all-gather(bf16[24,256]{1,0:T(8,128)(2,1)S(1)} %copy-done.82), channel_id=1, replica_groups=mesh['dp'=8,'seq'=4] {'dp','seq'}, dimensions={0}, use_global_device_ids=true | all-gather | bytes 405504 | tf_op jit(solution)/shard_map/all_gather | solution.py:153
  499.1 236.5 %gather_fusion = f32[65536,12]{1,0:T(8,128)} fusion(f32[12,1023]{0,1:T(8,128)S(1)} %fusion.83, s32[65536]{0:T(1024)} %broadcast_clamp_fusion), kind=kCustom, calls=%fused_computation | custom fusion | bytes 6553600 | tf_op jit(solution)/shard_map/jvp()/gather | solution.py:194
  735.6 20.9 copy.164
  769.8 8.1 copy.166
  777.9 6.2 copy.165
  784.1 6.3 copy.167
  790.8 64.9 %while.30 = (s32[]{:T(128)}, bf16[6,8,128,2,64]{2,4,3,1,0:T(8,128)(2,1)S(1)}, f32[6,8,2,128,1]{3,2,1,4,0:T(2,128)}, s32[6]{0:T(128)S(1)}, bf16[8,512,6,2,64]{1,4...) while((s32[]{:T(128)}, ...), condition=%wide.region_6.7_spmd.clone, body=%wide.region_3.6_spmd.clone.sunk | while | flops 284166144 | bytes 18171100 | solution.py:230
  864.0 38.3 %multiply_convert_fusion.3 = (bf16[1024,3072]{1,0:T(8,128)(2,1)}, f32[1024,3072]{1,0:T(8,128)}, f32[1024,3072]{1,0:T(8,128)}) fusion(f32[3072]{0:T(1024)S(1)} %convert_element_type.231, bf16[768,3072]{1,0:T(8,128)(2,1)} %all-gather.22.cloned.1.call-done, f32[1024,768]{1,0:T(8,128)} %copy-done.5, f32[768]{0:T(1024)S(1)} %convert_element_type.229, ...), kind=kOutput, calls=%fused_computation.72 | convolution fusion | flops 5043388416 | bytes 39348224 | tf_op jit(solution)/shard_map/dot_general | solution.py:53
  902.3 8.6 add_convert_fusion.2
  913.6 5.9 convolution_convert_fusion
  919.6 5.8 fusion.97
  933.0 19.3 convert_reduce_fusion
  952.3 9.8 multiply_reduce_fusion.1
  968.6 5.6 reshape.585
  974.2 6.1 copy.174
  980.7 224.3 %while.31 = (s32[]{:T(128)}, bf16[6,8,128,2,64]{2,4,3,1,0:T(8,128)(2,1)S(1)}, bf16[6,8,512,2,64]{2,4,3,0,1:T(8,128)(2,1)}, bf16[6,8,512,2,64]{2,4,3,0,1:T(8,128)...) while((s32[]{:T(128)}, ...), condition=%wide.region_21.22_spmd.clone, body=%wide.region_18.21_spmd.clone.sunk | while | flops 690892288 | bytes 83396904 | solution.py:355
  993.9 7.2 fusion.226
  1001.2 7.9 bitcast_dynamic-update-slice_fusion.9
  1031.3 7.2 fusion.226
  1038.5 7.9 bitcast_dynamic-update-slice_fusion.9
  1068.6 7.2 fusion.226
  1075.9 7.9 bitcast_dynamic-update-slice_fusion.9
  1106.0 7.2 fusion.226
  1113.2 7.9 bitcast_dynamic-update-slice_fusion.9
  1143.3 7.3 fusion.226
  1150.7 7.9 bitcast_dynamic-update-slice_fusion.9
  1180.7 7.2 fusion.226
  1187.9 7.9 bitcast_dynamic-update-slice_fusion.9
  1205.0 9.9 copy.202
  1214.9 7.4 copy.249
  1222.4 9.5 copy.204
  1231.8 7.4 copy.251
  1266.8 10.9 fusion.125
  1279.2 10.3 fusion.137
  1289.6 43.7 %reduce-scatter.34.cloned.1.call-done = bf16[128,6144]{1,0:T(8,128)(2,1)} async-done(((bf16[512,6144]{1,0:T(8,128)(2,1)}), bf16[128,6144]{1,0:T(8,128)(2,1)}) %reduce-scatter.34.cloned.1.call-update) | async-done | bytes 1572880
  1339.2 18.7 copy.188
  1357.9 347.6 %scatter_custom_fusion = f32[12,1023]{0,1:T(8,128)S(1)} fusion(s32[65536]{0:T(1024)} %bitcast.341, f32[65536,12]{1,0:T(8,128)} %bitcast.309, f32[]{:T(128)} %constant.79.clone.1), kind=kCustom, calls=%fused_computation.185 | custom fusion | flops 786432 | bytes 49616 | tf_op jit(solution)/shard_map/transpose(jvp())/scatter-add | solution.py:194
  1738.3 43.5 %all-reduce.26 = (f32[768]{0:T(1024)}, f32[768]{0:T(1024)}, f32[768]{0:T(1024)}, f32[768]{0:T(1024)}, f32[768]{0:T(1024)}, /*index=5*/f32[768]{0:T(1024)}, f32[3...) all-reduce(f32[768]{0:T(1024)} %get-tuple-element.428, ...), channel_id=5, replica_groups=mesh['dp'=8,'seq'=4] {'dp','seq'}, use_global_device_ids=true, to_apply=%region_32.33.clone | all-reduce | flops 14080 | bytes 112640
  1801.7 84.3 %reduce-scatter.26.cloned.1.call-done = f32[24,768]{1,0:T(8,128)} async-done(((f32[768,768]{1,0:T(8,128)}), f32[24,768]{1,0:T(8,128)}) %reduce-scatter.26.cloned.1.call-update) | async-done | bytes 73744 | tf_op jit(solution)/shard_map/reduce_scatter | solution.py:393
  1885.9 100.8 %reduce-scatter.38.cloned.1.call-done = f32[24,200]{1,0:T(8,128)} async-done(((f32[768,200]{1,0:T(8,128)}), f32[24,200]{1,0:T(8,128)}) %reduce-scatter.38.cloned.1.call-update) | async-done | bytes 19216
  1986.8 142.1 %reduce-scatter.28.cloned.1.call-done = f32[24,3072]{1,0:T(8,128)} async-done(((f32[768,3072]{1,0:T(8,128)}), f32[24,3072]{1,0:T(8,128)}) %reduce-scatter.28.cloned.1.call-update) | async-done | bytes 294928 | tf_op jit(solution)/shard_map/reduce_scatter | solution.py:400
  2128.8 141.1 %reduce-scatter.30.cloned.1.call-done = f32[96,768]{1,0:T(8,128)} async-done(((f32[3072,768]{1,0:T(8,128)}), f32[96,768]{1,0:T(8,128)}) %reduce-scatter.30.cloned.1.call-update) | async-done | bytes 294928 | tf_op jit(solution)/shard_map/reduce_scatter | solution.py:402
  2270.0 104.8 %reduce-scatter.22.cloned.1.call-done = f32[24,768]{1,0:T(8,128)} async-done(((f32[768,768]{1,0:T(8,128)}), f32[24,768]{1,0:T(8,128)}) %reduce-scatter.22.cloned.1.call-update) | async-done | bytes 73744 | tf_op jit(solution)/shard_map/reduce_scatter | solution.py:390
  2374.7 103.9 %reduce-scatter.24.cloned.1.call-done = f32[24,768]{1,0:T(8,128)} async-done(((f32[768,768]{1,0:T(8,128)}), f32[24,768]{1,0:T(8,128)}) %reduce-scatter.24.cloned.1.call-update) | async-done | bytes 73744 | tf_op jit(solution)/shard_map/reduce_scatter | solution.py:391
  (541 shorter events, 344.3 us)
Async XLA Ops:
  7.2 151.9 %copy-start.1 = (bf16[8,128,768]{2,1,0:T(8,128)(2,1)S(1)}, bf16[8,128,768]{2,1,0:T(8,128)(2,1)}, u32[]{:S(2)}) copy-start(bf16[8,128,768]{2,1,0:T(8,128)(2,1)} %param.33) | copy-start | bytes 4718596
  7.2 146.7 %all-reduce.33.cloned.1.call-start = ((), (), s32[]{:S(2)}) async-start(), calls=%async_computation.32 | async-start | bytes 168960
  19.2 194.4 %all-gather.10.cloned.1.call-start = ((), (), s32[]{:S(2)}) async-start(), calls=%async_computation.11 | async-start | bytes 1216512 | tf_op jit(solution)/shard_map/all_gather | solution.py:132
  19.9 249.5 %all-gather.16.cloned.1.call-start = ((), (), s32[]{:S(2)}) async-start(), calls=%async_computation.14 | async-start | bytes 1216512 | tf_op jit(solution)/shard_map/all_gather | solution.py:131
  20.7 742.9 %all-gather.14.cloned.1.call-start = ((), (), s32[]{:S(2)}) async-start(), calls=%async_computation.13 | async-start | bytes 1216512 | tf_op jit(solution)/shard_map/all_gather | solution.py:129
  21.2 756.7 %all-gather.12.cloned.1.call-start = ((), (), s32[]{:S(2)}) async-start(), calls=%async_computation.12 | async-start | bytes 7864320 | tf_op jit(solution)/shard_map/all_gather | solution.py:179
  23.8 137.3 %copy-start.85 = (pred[8,512]{1,0:T(8,128)(4,1)}, pred[8,512]{1,0:T(8,128)(4,1)S(1)}, u32[]{:S(2)}) copy-start(pred[8,512]{1,0:T(8,128)(4,1)S(1)} %fusion.107) | copy-start | bytes 12292
  23.8 137.3 %copy-start.79 = (pred[8,128]{1,0:T(8,128)(4,1)}, pred[8,128]{1,0:T(8,128)(4,1)S(1)}, u32[]{:S(2)}) copy-start(pred[8,128]{1,0:T(8,128)(4,1)S(1)} %constant_dynamic-slice_fusion) | copy-start | bytes 3076
  23.9 834.3 %copy-start.74 = (pred[1024]{0:T(1024)(128)(4,1)}, pred[1024]{0:T(1024)(128)(4,1)S(1)}, u32[]{:S(2)}) copy-start(pred[1024]{0:T(1024)(128)(4,1)S(1)} %fusion.193) | copy-start | bytes 3076
  155.9 702.2 %copy-start.44 = (f32[768]{0:T(1024)}, f32[768]{0:T(1024)S(1)}, u32[]{:S(2)}) copy-start(f32[768]{0:T(1024)S(1)} %convert_element_type.213) | copy-start | bytes 9220
  158.5 58.9 %copy-start.60 = (f32[1024]{0:T(1024)}, f32[1024]{0:T(1024)S(1)}, u32[]{:S(2)}) copy-start(f32[1024]{0:T(1024)S(1)} %get-tuple-element.516) | copy-start | bytes 12292
  159.9 57.4 %copy-start.54 = (f32[8,128]{1,0:T(8,128)}, f32[8,128]{1,0:T(8,128)S(1)}, u32[]{:S(2)}) copy-start(f32[8,128]{1,0:T(8,128)S(1)} %multiply_reduce_fusion.6) | copy-start | bytes 12292
  159.9 57.4 %copy-start.62 = (f32[1024]{0:T(1024)}, f32[1024]{0:T(1024)S(1)}, u32[]{:S(2)}) copy-start(f32[1024]{0:T(1024)S(1)} %bitcast_rsqrt_fusion) | copy-start | bytes 12292
  161.1 108.3 %copy-start.29 = (bf16[1024,768]{1,0:T(8,128)(2,1)}, bf16[1024,768]{1,0:T(8,128)(2,1)S(1)}, u32[]{:S(2)}) copy-start(bf16[1024,768]{1,0:T(8,128)(2,1)S(1)} %add_convert_fusion.6) | copy-start | bytes 4718596
  220.0 564.2 %all-gather.18.cloned.1.call-start = ((), (), s32[]{:S(2)}) async-start(), calls=%async_computation.15 | async-start | bytes 7864320 | tf_op jit(solution)/shard_map/all_gather | solution.py:178
  275.9 582.3 %all-gather.20.cloned.1.call-start = ((), (), s32[]{:S(2)}) async-start(), calls=%async_computation.16 | async-start | bytes 1216512 | tf_op jit(solution)/shard_map/all_gather | solution.py:134
  276.6 587.3 %all-gather.22.cloned.1.call-start = ((), (), s32[]{:S(2)}) async-start(), calls=%async_computation.17 | async-start | bytes 4866048 | tf_op jit(solution)/shard_map/all_gather | solution.py:143
  277.4 624.9 %all-gather.24.cloned.1.call-start = ((), (), s32[]{:S(2)}) async-start(), calls=%async_computation.18 | async-start | bytes 4866048 | tf_op jit(solution)/shard_map/all_gather | solution.py:145
  278.1 635.5 %all-gather.26.cloned.1.call-start = ((), (), s32[]{:S(2)}) async-start(), calls=%async_computation.19 | async-start | bytes 2621440 | tf_op jit(solution)/shard_map/all_gather | solution.py:265
  278.4 219.3 %copy-start.32 = (s32[16,4,8,128]{3,1,2,0:T(4,128)}, s32[16,4,8,128]{3,1,2,0:T(4,128)S(1)}, u32[]{:S(2)}) copy-start(s32[16,4,8,128]{3,1,2,0:T(4,128)S(1)} %copy.245) | copy-start | bytes 786436
  352.8 145.7 %copy-start.104 = (bf16[768]{0:T(1024)(128)(2,1)S(1)}, bf16[768]{0:T(1024)(128)(2,1)}, u32[]{:S(2)}) copy-start(bf16[768]{0:T(1024)(128)(2,1)} %get-tuple-element.486) | copy-start | bytes 4612
  352.8 145.7 %copy-start.103 = (bf16[768]{0:T(1024)(128)(2,1)S(1)}, bf16[768]{0:T(1024)(128)(2,1)}, u32[]{:S(2)}) copy-start(bf16[768]{0:T(1024)(128)(2,1)} %get-tuple-element.491) | copy-start | bytes 4612
  352.8 145.7 %copy-start.86 = (bf16[3840]{0:T(1024)(128)(2,1)S(1)}, bf16[3840]{0:T(1024)(128)(2,1)}, u32[]{:S(2)}) copy-start(bf16[3840]{0:T(1024)(128)(2,1)} %get-tuple-element.492) | copy-start | bytes 23044
  352.8 145.8 %copy-start.97 = (s32[1023]{0:T(1024)S(1)}, s32[1023]{0:T(1024)}, u32[]{:S(2)}) copy-start(s32[1023]{0:T(1024)} %param.40) | copy-start | bytes 12280
  352.9 382.6 %copy-start.3 = (f32[1024,2,100]{0,2,1:T(8,128)}, f32[1024,2,100]{0,2,1:T(8,128)S(1)}, u32[]{:S(2)}) copy-start(f32[1024,2,100]{0,2,1:T(8,128)S(1)} %reshape.525) | copy-start | bytes 2457604
  353.0 145.5 %copy-start.37 = (f32[1024,2]{0,1:T(2,128)}, f32[1024,2]{0,1:T(2,128)S(1)}, u32[]{:S(2)}) copy-start(f32[1024,2]{0,1:T(2,128)S(1)} %reduce_max.27) | copy-start | bytes 24580
  353.2 145.3 %copy-start.41 = (f32[1024,2]{0,1:T(2,128)}, f32[1024,2]{0,1:T(2,128)S(1)}, u32[]{:S(2)}) copy-start(f32[1024,2]{0,1:T(2,128)S(1)} %fusion.102) | copy-start | bytes 24580
  497.7 260.1 %copy-start.22 = (bf16[1024,2,100]{0,2,1:T(8,128)(2,1)}, bf16[1024,2,100]{0,2,1:T(8,128)(2,1)S(1)}, u32[]{:S(2)}) copy-start(bf16[1024,2,100]{0,2,1:T(8,128)(2,1)S(1)} %divide_convert_fusion.7) | copy-start | bytes 1228804
  756.6 107.4 %copy-start.83 = (f32[3072]{0:T(1024)}, f32[3072]{0:T(1024)S(1)}, u32[]{:S(2)}) copy-start(f32[3072]{0:T(1024)S(1)} %convert_element_type.231) | copy-start | bytes 36868
  756.6 107.4 %copy-start.52 = (f32[768]{0:T(1024)}, f32[768]{0:T(1024)S(1)}, u32[]{:S(2)}) copy-start(f32[768]{0:T(1024)S(1)} %convert_element_type.229) | copy-start | bytes 9220
  756.6 205.5 %copy-start.47 = (f32[768]{0:T(1024)}, f32[768]{0:T(1024)S(1)}, u32[]{:S(2)}) copy-start(f32[768]{0:T(1024)S(1)} %convert_element_type.228) | copy-start | bytes 9220
  763.5 475.9 %reduce-scatter.18.cloned.1.call-start = ((), (), s32[]{:S(2)}) async-start(), calls=%async_computation.20 | async-start | bytes 2621440 | tf_op jit(solution)/shard_map/reduce_scatter | solution.py:281
  861.7 100.4 %copy-start.35 = (f32[1024]{0:T(1024)}, f32[1024]{0:T(1024)S(1)}, u32[]{:S(2)}) copy-start(f32[1024]{0:T(1024)S(1)} %broadcast_multiply_fusion) | copy-start | bytes 12292
  863.9 98.2 %copy-start.39 = (f32[1024]{0:T(1024)}, f32[1024]{0:T(1024)S(1)}, u32[]{:S(2)}) copy-start(f32[1024]{0:T(1024)S(1)} %fusion.111) | copy-start | bytes 12292
  919.6 413.7 %reduce-scatter.34.cloned.1.call-start = ((), (), s32[]{:S(2)}) async-start(), calls=%async_computation.28 | async-start | bytes 7864320
  1205.0 47.9 %copy-start.13 = (bf16[6,8,128,2,64]{2,4,3,1,0:T(8,128)(2,1)}, bf16[6,8,128,2,64]{2,4,3,1,0:T(8,128)(2,1)S(1)}, u32[]{:S(2)}) copy-start(bf16[6,8,128,2,64]{2,4,3,1,0:T(8,128)(2,1)S(1)} %get-tuple-element.143) | copy-start | bytes 4718596
  1222.3 489.5 %reduce-scatter.36.cloned.1.call-start = ((), (), s32[]{:S(2)}) async-start(), calls=%async_computation.29 | async-start | bytes 7864320
  1239.3 486.1 %all-reduce.31.cloned.1.call-start = ((), (), s32[]{:S(2)}) async-start(), calls=%async_computation.31 | async-start | bytes 204800
  1248.2 553.4 %reduce-scatter.32.cloned.1.call-start = ((), (), s32[]{:S(2)}) async-start(), calls=%async_computation.27 | async-start | bytes 811008 | tf_op jit(solution)/shard_map/reduce_scatter | solution.py:408
  1251.8 549.8 %reduce-scatter.20.cloned.1.call-start = ((), (), s32[]{:S(2)}) async-start(), calls=%async_computation.21 | async-start | bytes 2433024 | tf_op jit(solution)/shard_map/reduce_scatter | solution.py:388
  1258.3 627.6 %reduce-scatter.26.cloned.1.call-start = ((), (), s32[]{:S(2)}) async-start(), calls=%async_computation.24 | async-start | bytes 2433024 | tf_op jit(solution)/shard_map/reduce_scatter | solution.py:393
  1263.7 723.1 %reduce-scatter.38.cloned.1.call-start = ((), (), s32[]{:S(2)}) async-start(), calls=%async_computation.30 | async-start | bytes 811008
  1266.7 862.1 %reduce-scatter.28.cloned.1.call-start = ((), (), s32[]{:S(2)}) async-start(), calls=%async_computation.25 | async-start | bytes 9732096 | tf_op jit(solution)/shard_map/reduce_scatter | solution.py:400
  1277.8 992.2 %reduce-scatter.30.cloned.1.call-start = ((), (), s32[]{:S(2)}) async-start(), calls=%async_computation.26 | async-start | bytes 9732096 | tf_op jit(solution)/shard_map/reduce_scatter | solution.py:402
  1289.5 1085.2 %reduce-scatter.22.cloned.1.call-start = ((), (), s32[]{:S(2)}) async-start(), calls=%async_computation.22 | async-start | bytes 2433024 | tf_op jit(solution)/shard_map/reduce_scatter | solution.py:390
  1339.1 1139.5 %reduce-scatter.24.cloned.1.call-start = ((), (), s32[]{:S(2)}) async-start(), calls=%async_computation.23 | async-start | bytes 2433024 | tf_op jit(solution)/shard_map/reduce_scatter | solution.py:391
  1339.2 366.4 %copy-start.98 = (s32[1023]{0:T(1024)S(1)}, s32[1023]{0:T(1024)}, u32[]{:S(2)}) copy-start(s32[1023]{0:T(1024)} %param.40) | copy-start | bytes 12280
  1736.7 60.2 %copy-start.10 = (f32[1024,768]{1,0:T(8,128)S(1)}, f32[1024,768]{1,0:T(8,128)}, u32[]{:S(2)}) copy-start(f32[1024,768]{1,0:T(8,128)} %copy-done.8) | copy-start | bytes 9437188
  (92 other events, 585.1 us)
Sparse Core Ops, SparseCore 0:
  19.3 134.5 all-reduce.32
  158.0 55.4 all-gather.9
  216.3 53.0 all-gather.15
  272.1 53.2 all-gather.13
  326.7 119.4 all-gather.11
  447.6 114.8 all-gather.17
  565.3 54.1 all-gather.19
  622.2 62.4 all-gather.21
  687.6 62.3 all-gather.23
  763.6 46.0 all-gather.25
  919.7 43.9 reduce-scatter.17
  1222.4 110.8 reduce-scatter.33
  1335.7 111.2 reduce-scatter.35
  1453.4 121.1 all-reduce.30
  1580.9 96.3 reduce-scatter.31
  1683.9 98.2 reduce-scatter.19
  1787.9 98.0 reduce-scatter.25
  1892.3 94.4 reduce-scatter.37
  1994.3 134.5 reduce-scatter.27
  2135.2 134.7 reduce-scatter.29
  2276.7 97.9 reduce-scatter.21
  2380.6 98.0 reduce-scatter.23
where the time goes:
time: 2500 us; the launch traced here: 2490 us
  waiting for transfers between devices  957 us (38%)
  local copies, waits for them, and re-layouts  445 us (18%)
  other arithmetic  420 us (17%)
  matrix products  363 us (15%)
  blocking collectives  258 us (10%)
    scatter-add x1, other arithmetic, local_bias(): return per_offset[:, offsets]  348 us
    unnamed x27, waiting for transfers between devices  279 us
    gather x2, local copies, waits for them, and re-layouts, local_bias(): return per_offset[:, offsets]  257 us
    all_gather x1, blocking collectives, head_weights(): lax.all_gather(contrast_space_map, ('dp', 'seq'), axis=0, tiled=True)  144 us
    reduce_scatter x1, waiting for transfers between devices, body(): lax.psum_scatter(inner_weight_grad, ('dp', 'seq'), scatter_dimension=0, t...  142 us
    reduce_scatter x1, waiting for transfers between devices, body(): lax.psum_scatter(outer_weight_grad, ('dp', 'seq'), scatter_dimension=0, t...  141 us
    unnamed x280, local copies, waits for them, and re-layouts  111 us
    reduce_scatter x1, waiting for transfers between devices, body(): lax.psum_scatter(key_weight_grad, ('dp', 'seq'), scatter_dimension=0, til...  105 us
  transfers between devices with their start and end apart: 22, of which 10 were waited for; matrix products, arithmetic and copies ran while one was open for 48% of the time, Pallas kernels for 0%

commit v1 on v0

v1 whole, which is shorter than its diff:
```python
import functools
import math

import jax
import jax.numpy as jnp
from jax import lax
from jax.experimental import pallas as pl
from jax.experimental.pallas import tpu as pltpu
from jax.sharding import PartitionSpec as P

D = 768
H = 12
HD = 64
FF = 3072
NB = 320
CODE_GROUPS = 2
GROUP_CODES = 100
CDG = 128
CD = CODE_GROUPS * CDG
CODES = CODE_GROUPS * GROUP_CODES
F = 512
PAIRS = H // 2
SPAN = 1024
EPSILON = 1e-05
CONTRAST_SCALE = 0.05
NEGATIVE = -1000000000.0
HIGHEST = lax.Precision.HIGHEST
F32 = jnp.float32
BF16 = jnp.bfloat16


def dot_nt(a, b):
    return lax.dot_general(a, b, (((1,), (1,)), ((), ())), preferred_element_type=F32)


def dot_nn(a, b):
    return lax.dot_general(a, b, (((1,), (0,)), ((), ())), preferred_element_type=F32)


def dot_tn(a, b):
    return lax.dot_general(a, b, (((0,), (0,)), ((), ())), preferred_element_type=F32)


def spread_table(w_ref, g_ref):
    for a in range(2):
        row = jnp.broadcast_to(w_ref[0, a : a + 1, :], (128, SPAN))
        g_ref[a] = pltpu.roll(row, SPAN - 127, 1, stride=1, stride_axis=0)


def biased(scores, g_ref, a, mask_col):
    tiles = [
        scores[128 * b : 128 * b + 128] + g_ref[a, :, 384 - 128 * b : 896 - 128 * b]
        for b in range(F // 128)
    ]
    return jnp.concatenate(tiles, axis=0) + mask_col


def attend_kernel(qkv_ref, mask_ref, w_ref, mixed_ref, total_ref, g_ref):
    @pl.when(pl.program_id(1) == 0)
    def _():
        spread_table(w_ref, g_ref)

    q, k, v = qkv_ref[:, 0:128], qkv_ref[:, 128:256], qkv_ref[:, 256:384]
    first = lax.broadcasted_iota(jnp.int32, (F, 128), 1) < HD
    q8 = q * jnp.asarray(1.0 / math.sqrt(HD), q.dtype)
    zero = jnp.zeros_like(q)
    mask_col = mask_ref[...]
    turned = []
    for a in range(2):
        qa = jnp.where(first if a == 0 else ~first, q8, zero)
        scores = biased(dot_nt(k, qa), g_ref, a, mask_col)
        top = jnp.max(scores, axis=0, keepdims=True)
        terms = jnp.exp(scores - top)
        total = jnp.sum(terms, axis=0, keepdims=True)
        out = dot_tn(v, terms.astype(BF16))
        turned.append((out * (1.0 / total))[HD * a : HD * a + HD])
        total_ref[0, 0, a : a + 1, :] = top + jnp.log(total)
    mixed_ref[...] = jnp.concatenate(turned, axis=0).T.astype(BF16)


def attend(qkv, key_shift, per_offset):
    own = qkv.shape[0] // F
    return pl.pallas_call(
        attend_kernel,
        grid=(PAIRS, own),
        in_specs=[
            pl.BlockSpec((F, 384), lambda p, u: (u, p)),
            pl.BlockSpec((F, 1), lambda p, u: (u, 0)),
            pl.BlockSpec((1, 2, SPAN), lambda p, u: (p, 0, 0)),
        ],
        out_specs=[
            pl.BlockSpec((F, 128), lambda p, u: (u, p)),
            pl.BlockSpec((1, 1, 2, F), lambda p, u: (p, u, 0, 0)),
        ],
        out_shape=[
            jax.ShapeDtypeStruct((own * F, D), BF16),
            jax.ShapeDtypeStruct((PAIRS, own, 2, F), F32),
        ],
        scratch_shapes=[pltpu.VMEM((2, 128, SPAN), F32)],
        compiler_params=pltpu.CompilerParams(vmem_limit_bytes=40 * 1024 * 1024),
        cost_estimate=pl.CostEstimate(
            flops=own * H * 2 * F * F * 256 * 6, bytes_accessed=10_000_000, transcendentals=0
        ),
        name="attend",
    )(qkv, key_shift, per_offset)


def attend_back_kernel(
    own, qkv_ref, grad_ref, total_ref, mask_ref, w_ref, low_ref, dw_ref, g_ref, dg_ref
):
    u = pl.program_id(1)

    @pl.when(u == 0)
    def _():
        spread_table(w_ref, g_ref)
        dg_ref[...] = jnp.zeros_like(dg_ref)

    q, k, v = qkv_ref[:, 0:128], qkv_ref[:, 128:256], qkv_ref[:, 256:384]
    grad = grad_ref[...]
    first = lax.broadcasted_iota(jnp.int32, (F, 128), 1) < HD
    scale = 1.0 / math.sqrt(HD)
    q8 = q * jnp.asarray(scale, q.dtype)
    zero = jnp.zeros_like(q)
    mask_col = mask_ref[...]
    dk = jnp.zeros((F, 128), F32)
    dv = jnp.zeros((F, 128), F32)
    dq = jnp.zeros((128, F), F32)
    for a in range(2):
        pick = first if a == 0 else ~first
        qa, ka, ga = jnp.where(pick, q8, zero), jnp.where(pick, k, zero), jnp.where(pick, grad, zero)
        scores = biased(dot_nt(k, qa), g_ref, a, mask_col)
        probs = jnp.exp(scores - total_ref[0, 0, a : a + 1, :])
        probs_grad = dot_nt(v, ga)
        spread = jnp.sum(probs * probs_grad, axis=0, keepdims=True)
        score_grad = probs * (probs_grad - spread)
        for b in range(F // 128):
            lo = 384 - 128 * b
            dg_ref[a, :, lo : lo + F] += score_grad[128 * b : 128 * b + 128]
        low = score_grad.astype(BF16)
        dv += dot_nn(probs.astype(BF16), ga)
        dk += dot_nn(low, qa)
        dq += dot_tn(ka, low)
    low_ref[:, 0:128] = (dq.T * scale).astype(BF16)
    low_ref[:, 128:256] = dk.astype(BF16)
    low_ref[:, 256:384] = dv.astype(BF16)

    @pl.when(u == own - 1)
    def _():
        for a in range(2):
            x = dg_ref[a]
            n = 64
            while n >= 1:
                x = x[:n] + pltpu.roll(x[n:], SPAN - n, 1)
                n //= 2
            dw_ref[0, a : a + 1, :] = pltpu.roll(x, 127, 1)


def attend_back(qkv, grad, log_totals, key_shift, per_offset):
    own = qkv.shape[0] // F
    return pl.pallas_call(
        functools.partial(attend_back_kernel, own),
        grid=(PAIRS, own),
        in_specs=[
            pl.BlockSpec((F, 384), lambda p, u: (u, p)),
            pl.BlockSpec((F, 128), lambda p, u: (u, p)),
            pl.BlockSpec((1, 1, 2, F), lambda p, u: (p, u, 0, 0)),
            pl.BlockSpec((F, 1), lambda p, u: (u, 0)),
            pl.BlockSpec((1, 2, SPAN), lambda p, u: (p, 0, 0)),
        ],
        out_specs=[
            pl.BlockSpec((F, 384), lambda p, u: (u, p)),
            pl.BlockSpec((1, 2, SPAN), lambda p, u: (p, 0, 0)),
        ],
        out_shape=[
            jax.ShapeDtypeStruct((own * F, 3 * D), BF16),
            jax.ShapeDtypeStruct((PAIRS, 2, SPAN), F32),
        ],
        scratch_shapes=[pltpu.VMEM((2, 128, SPAN), F32), pltpu.VMEM((2, 128, SPAN), F32)],
        compiler_params=pltpu.CompilerParams(vmem_limit_bytes=40 * 1024 * 1024),
        cost_estimate=pl.CostEstimate(
            flops=own * H * 5 * F * F * 256 * 4, bytes_accessed=14_000_000, transcendentals=0
        ),
        name="attend_back",
    )(qkv, grad, log_totals, key_shift, per_offset)


def contrast_kernel(projected_ref, target_ref, col_ref, row_ref, low_ref, unit_ref):
    projected = projected_ref[...]
    r = lax.rsqrt(jnp.sum(projected * projected, axis=-1, keepdims=True) + EPSILON)
    unit = (projected * r).astype(BF16)
    target = target_ref[...]
    logits = jnp.where(
        col_ref[...] > 0.5, dot_nt(target, unit) * (1.0 / CONTRAST_SCALE), NEGATIVE
    )
    terms = jnp.exp(logits - jnp.max(logits, axis=0, keepdims=True))
    total = jnp.sum(terms, axis=0, keepdims=True)
    own_hits = lax.broadcasted_iota(jnp.int32, (F, F), 0) == lax.broadcasted_iota(
        jnp.int32, (F, F), 1
    )
    weight = row_ref[0] * (1.0 / CONTRAST_SCALE)
    low = (terms * (weight / total) - jnp.where(own_hits, weight, 0.0)).astype(BF16)
    unit_ref[...] = dot_nn(low, unit).astype(BF16)
    grad = dot_tn(low, target)
    inner = jnp.sum(grad * projected, axis=-1, keepdims=True)
    low_ref[...] = (r * grad - projected * (r * r * r * inner)).astype(BF16)


def contrast(projected, targets, mask_col, mask_row):
    own = projected.shape[0] // F
    return pl.pallas_call(
        contrast_kernel,
        grid=(own,),
        in_specs=[
            pl.BlockSpec((F, CD), lambda u: (u, 0)),
            pl.BlockSpec((F, CD), lambda u: (u, 0)),
            pl.BlockSpec((F, 1), lambda u: (u, 0)),
            pl.BlockSpec((1, 1, F), lambda u: (u, 0, 0)),
        ],
        out_specs=[
            pl.BlockSpec((F, CD), lambda u: (u, 0)),
            pl.BlockSpec((F, CD), lambda u: (u, 0)),
        ],
        out_shape=[jax.ShapeDtypeStruct((own * F, CD), BF16)] * 2,
        compiler_params=pltpu.CompilerParams(vmem_limit_bytes=40 * 1024 * 1024),
        cost_estimate=pl.CostEstimate(
            flops=own * 6 * F * F * 256 * 4, bytes_accessed=4_000_000, transcendentals=0
        ),
        name="contrast",
    )(projected, targets, mask_col, mask_row)


class Grid:
    def __init__(self, mesh):
        dp, seq = mesh.shape["dp"], mesh.shape["seq"]
        dims = []
        left = dp
        while left > 1:
            size = 4 if left % 4 == 0 else 2
            left //= size
            dims.append(("dp", size, left))
        dims.append(("seq", seq, 1))
        self.dims = dims
        self.sizes = tuple(size for _, size, _ in dims)
        self.total = dp * seq
        self.extent = {"dp": dp, "seq": seq}

    def place(self, j):
        axis, size, stride = self.dims[j]
        return (lax.axis_index(axis) // stride) % size

    def swap(self, j, d, value):
        axis, size, stride = self.dims[j]
        pairs = [(i, i ^ (d * stride)) for i in range(self.extent[axis])]
        return lax.ppermute(value, axis, pairs)

    def gather_order(self):
        n = len(self.dims)
        return [n - 1] + list(range(n - 1))


def gather_rows(grid, block):
    n = len(grid.dims)
    buf = block.reshape((1,) * n + block.shape)
    for j in grid.gather_order():
        size = grid.sizes[j]
        me = grid.place(j)
        parts = [buf] + [grid.swap(j, d, buf) for d in range(1, size)]
        shape = buf.shape[:j] + (size,) + buf.shape[j + 1 :]
        out = jnp.zeros(shape, buf.dtype)
        for d, part in enumerate(parts):
            out = lax.dynamic_update_slice_in_dim(out, part, me ^ d, axis=j)
        buf = out
    return buf.reshape((grid.total * block.shape[0],) + block.shape[1:])


def scatter_rows(grid, whole):
    n = len(grid.dims)
    rows = whole.shape[0] // grid.total
    buf = whole.reshape(grid.sizes + (rows,) + whole.shape[1:])
    order = grid.gather_order()[::-1]
    for step, j in enumerate(order):
        size = grid.sizes[j]
        me = grid.place(j)
        total = lax.dynamic_slice_in_dim(buf, me, 1, axis=j).astype(F32)
        for d in range(1, size):
            send = lax.dynamic_slice_in_dim(buf, me ^ d, 1, axis=j).astype(BF16)
            total = total + grid.swap(j, d, send).astype(F32)
        buf = total if step == n - 1 else total.astype(BF16)
    return buf.reshape((rows,) + whole.shape[1:])


def to_utterances(grid, value):
    j = len(grid.dims) - 1
    size = grid.sizes[j]
    me = grid.place(j)
    utts, here, wide = value.shape
    own = utts // size
    blocks = value.reshape(size, own, here, wide)
    out = jnp.zeros((own, size, here, wide), value.dtype)
    for d in range(size):
        part = lax.dynamic_index_in_dim(blocks, me ^ d, 0, keepdims=False)
        if d:
            part = grid.swap(j, d, part)
        out = lax.dynamic_update_slice_in_dim(out, part[:, None], me ^ d, axis=1)
    return out.reshape(own, size * here, wide)


def to_frames(grid, value):
    j = len(grid.dims) - 1
    size = grid.sizes[j]
    me = grid.place(j)
    own, frames, wide = value.shape
    here = frames // size
    blocks = value.reshape(own, size, here, wide)
    out = jnp.zeros((size, own, here, wide), value.dtype)
    for d in range(size):
        part = lax.dynamic_index_in_dim(blocks, me ^ d, 1, keepdims=False)
        if d:
            part = grid.swap(j, d, part)
        out = lax.dynamic_update_slice_in_dim(out, part[None], me ^ d, axis=0)
    return out.reshape(size * own, here, wide)


def as_columns(vector, rows):
    count = -(-vector.shape[0] // rows)
    flat = jnp.pad(vector, (0, rows * count - vector.shape[0]))
    return flat.reshape(rows, count)


def norm_stats(values):
    mean = jnp.mean(values, axis=-1, keepdims=True)
    centred = values - mean
    variance = jnp.mean(centred * centred, axis=-1, keepdims=True)
    inverse = lax.rsqrt(variance + EPSILON)
    return centred * inverse, inverse


def norm_back(unit, inverse, gain, grad):
    scaled = grad * gain
    first = jnp.mean(scaled, axis=-1, keepdims=True)
    second = jnp.mean(scaled * unit, axis=-1, keepdims=True)
    gain_grad = jnp.sum(grad * unit, axis=0)
    shift_grad = jnp.sum(grad, axis=0)
    return (scaled - first - unit * second) * inverse, gain_grad, shift_grad


def unit_back(values, grad):
    r = lax.rsqrt(jnp.sum(values * values, axis=-1, keepdims=True) + EPSILON)
    return r * grad - values * (r * r * r) * jnp.sum(grad * values, axis=-1, keepdims=True)


def row_total(values):
    return jnp.sum(values.astype(F32), axis=0)


def group_reduce(values, reduce, fill):
    low = lax.broadcasted_iota(jnp.int32, values.shape, 1) < GROUP_CODES
    a = reduce(jnp.where(low, values, fill), axis=-1, keepdims=True)
    b = reduce(jnp.where(low, fill, values), axis=-1, keepdims=True)
    return jnp.where(low, a, b)


def body(
    grid,
    acoustic_features,
    upstream_derivative,
    flat_random_draws,
    softening_scalar,
    valid_frame_counts,
    hidden_run_beginnings,
    hidden_run_sizes,
    distance_bins,
    hidden_frame_vector,
    premix_scale_vector,
    premix_shift_vector,
    question_map,
    question_shift,
    lookup_address_map,
    content_map,
    content_shift,
    mixing_result_map,
    mixing_result_shift,
    distance_bin_shifts,
    premlp_scale_vector,
    premlp_shift_vector,
    perceptron_entry_map,
    perceptron_inner_shift,
    perceptron_final_map,
    perceptron_final_shift,
    codeword_score_map,
    codeword_vectors,
    contrast_space_map,
    contrast_space_shift,
):
    utts, here = acoustic_features.shape[:2]
    parts = grid.sizes[-1]
    own = utts // parts
    rows = own * F
    local_rows = utts * here
    me_seq = lax.axis_index("seq")
    shard = question_map.shape[0]

    def by_pairs(*maps):
        n = maps[0].shape[0]
        return jnp.stack([m.reshape(n, PAIRS, 128) for m in maps], axis=2).reshape(n, -1)

    vectors = (
        hidden_frame_vector,
        premix_scale_vector,
        premix_shift_vector,
        question_shift,
        content_shift,
        mixing_result_shift,
        premlp_scale_vector,
        premlp_shift_vector,
        perceptron_final_shift,
        distance_bin_shifts,
        perceptron_inner_shift,
        contrast_space_shift,
        codeword_vectors,
    )
    packed = [as_columns(v, shard) for v in vectors]
    widths = [p.shape[1] for p in packed]
    small_width = -(-(CD + CODES + sum(widths)) // 128) * 128
    fill = jnp.zeros((shard, small_width - CD - CODES - sum(widths)), BF16)
    small = jnp.concatenate([contrast_space_map, codeword_score_map] + packed + [fill], axis=1)
    small_full = gather_rows(grid, small)
    qkv_map = gather_rows(grid, by_pairs(question_map, lookup_address_map, content_map))
    frames = to_utterances(grid, acoustic_features).reshape(rows, D)
    entry_full = gather_rows(
        grid, jnp.concatenate([mixing_result_map, perceptron_entry_map], axis=1)
    )
    final_map = gather_rows(grid, perceptron_final_map)
    contrast_map = small_full[:, :CD]
    score_map = small_full[:, CD : CD + CODES]
    flats = []
    at = CD + CODES
    turned = small_full[:, at:].T
    for v, w in zip(vectors, widths):
        lo = at - CD - CODES
        if w == 1 and v.shape[0] == shard:
            flats.append(turned[lo])
        else:
            cols = small_full[:, at : at + w].reshape(grid.total, shard * w)[:, : v.shape[0]]
            flats.append(cols.reshape(-1))
        at += w
    (
        mask_vector,
        gain_one,
        shift_one,
        query_bias,
        value_bias,
        mix_bias,
        gain_two,
        shift_two,
        final_bias,
        table,
        inner_bias,
        contrast_bias,
        codebook,
    ) = [f.astype(F32) for f in flats]
    mix_map = entry_full[:, :D]
    entry_map = entry_full[:, D:]

    local_frames = acoustic_features.reshape(local_rows, D)
    noise = -jnp.log(-jnp.log(flat_random_draws.reshape(local_rows, CODES)))
    temperature = softening_scalar[0]
    code_scores = (dot_nn(local_frames, score_map) + noise) / temperature
    code_terms = jnp.exp(code_scores - group_reduce(code_scores, jnp.max, -jnp.inf))
    code_probs = code_terms / group_reduce(code_terms, jnp.sum, 0.0)
    code_low = code_probs.astype(BF16)
    books = codebook.astype(BF16).reshape(CODE_GROUPS, GROUP_CODES, CDG)
    book_map = jnp.concatenate(
        [jnp.pad(books[g], ((0, 0), (g * CDG, CD - (g + 1) * CDG))) for g in range(CODE_GROUPS)],
        axis=0,
    )
    target_raw = dot_nn(code_low, book_map)
    target_unit = target_raw * lax.rsqrt(
        jnp.sum(target_raw * target_raw, axis=-1, keepdims=True) + EPSILON
    )
    targets = to_utterances(grid, target_unit.astype(BF16).reshape(utts, here, CD))
    targets = targets.reshape(rows, CD)
    upstream = to_utterances(grid, upstream_derivative).reshape(rows, D)

    def mine(v):
        return lax.dynamic_slice_in_dim(v, me_seq * own, own, 0)

    counts, starts, sizes = (
        mine(valid_frame_counts),
        mine(hidden_run_beginnings),
        mine(hidden_run_sizes),
    )
    at_frame = jnp.arange(F, dtype=jnp.int32)
    covered = jnp.any(
        (starts[:, :, None] <= at_frame) & (at_frame < (starts + sizes)[:, :, None]), axis=1
    )
    key_valid = at_frame[None, :] < counts[:, None]
    masked = covered & key_valid
    mask_rows = masked.reshape(rows, 1)
    key_shift = jnp.where(key_valid, 0.0, NEGATIVE).astype(F32).reshape(rows, 1)
    masked_f = masked.astype(F32)

    backwards = jnp.pad(distance_bins[::-1], (0, SPAN - distance_bins.shape[0]), constant_values=-1)
    bucket_hits = backwards[None, :] == jnp.arange(NB, dtype=jnp.int32)[:, None]
    per_offset = dot_nn(table.astype(BF16).reshape(H, NB), bucket_hits.astype(BF16))
    per_offset = per_offset.reshape(PAIRS, 2, SPAN)

    start = jnp.where(mask_rows, mask_vector[None, :], frames.astype(F32))
    start_unit, start_inverse = norm_stats(start)
    normed = (start_unit * gain_one + shift_one).astype(BF16)
    qkv_bias = by_pairs(
        query_bias[None], jnp.zeros_like(query_bias)[None], value_bias[None]
    )
    qkv = (dot_nn(normed, qkv_map) + qkv_bias).astype(BF16)
    mixed, log_totals = attend(qkv, key_shift, per_offset)
    middle = start + dot_nn(mixed, mix_map) + mix_bias
    middle_unit, middle_inverse = norm_stats(middle)
    normed_ffn = (middle_unit * gain_two + shift_two).astype(BF16)
    inner = dot_nn(normed_ffn, entry_map) + inner_bias
    cdf = 0.5 * (1.0 + lax.erf(inner * math.sqrt(0.5)))
    activated = (inner * cdf).astype(BF16)
    slope = (cdf + inner * jnp.exp(-0.5 * inner * inner) * (1.0 / math.sqrt(2 * math.pi))).astype(
        BF16
    )
    encoded = (middle + dot_nn(activated, final_map) + final_bias).astype(BF16)
    encoded_out = to_frames(grid, encoded.reshape(own, F, D))
    projected = dot_nn(encoded, contrast_map) + contrast_bias
    projected_low, unit_grad = contrast(
        projected, targets, masked_f.reshape(rows, 1), masked_f.reshape(own, 1, F)
    )

    unit_here = to_frames(grid, unit_grad.reshape(own, F, CD)).reshape(local_rows, CD)
    target_low = unit_back(target_raw, unit_here.astype(F32)).astype(BF16)
    book_grad = dot_tn(code_low, target_low)
    codebook_grad = jnp.stack(
        [
            book_grad[g * GROUP_CODES : (g + 1) * GROUP_CODES, g * CDG : (g + 1) * CDG]
            for g in range(CODE_GROUPS)
        ]
    ).reshape(-1)
    probs_grad = dot_nt(target_low, book_map)
    logits_low = (
        code_probs * (probs_grad - group_reduce(code_probs * probs_grad, jnp.sum, 0.0)) / temperature
    ).astype(BF16)
    score_map_grad = dot_tn(local_frames, logits_low)
    code_path = dot_nt(logits_low, score_map)

    contrast_map_grad = dot_tn(encoded, projected_low)
    contrast_bias_grad = row_total(projected_low)
    output_grad = upstream.astype(F32) + dot_nt(projected_low, contrast_map)
    branch_low = output_grad.astype(BF16)
    final_map_grad = dot_tn(activated, branch_low).astype(BF16)
    final_shard = scatter_rows(grid, final_map_grad)
    final_bias_grad = row_total(branch_low)
    inner_low = (dot_nt(branch_low, final_map) * slope.astype(F32)).astype(BF16)
    entry_map_grad = dot_tn(normed_ffn, inner_low).astype(BF16)
    entry_shard = scatter_rows(grid, entry_map_grad)
    inner_bias_grad = row_total(inner_low)
    middle_part, gain_two_grad, shift_two_grad = norm_back(
        middle_unit, middle_inverse, gain_two, dot_nt(inner_low, entry_map)
    )
    middle_grad = output_grad + middle_part
    attn_low = middle_grad.astype(BF16)
    mix_map_grad = dot_tn(mixed, attn_low).astype(BF16)
    mix_bias_grad = row_total(attn_low)
    mixed_low = dot_nt(attn_low, mix_map).astype(BF16)
    qkv_low, per_offset_grad = attend_back(qkv, mixed_low, log_totals, key_shift, per_offset)
    qkv_map_grad = dot_tn(normed, qkv_low).astype(BF16)
    qkv_bias_grad = row_total(qkv_low).reshape(PAIRS, 3, 128)
    start_part, gain_one_grad, shift_one_grad = norm_back(
        start_unit, start_inverse, gain_one, dot_nt(qkv_low, qkv_map)
    )
    start_grad = middle_grad + start_part
    mask_vector_grad = jnp.sum(jnp.where(mask_rows, start_grad, 0.0), axis=0)
    open_grad = jnp.where(mask_rows, 0.0, start_grad).astype(BF16)
    frames_grad = (
        to_frames(grid, open_grad.reshape(own, F, D)).astype(F32)
        + code_path.reshape(utts, here, D)
    )
    table_grad = lax.dot_general(
        per_offset_grad.reshape(H, SPAN),
        bucket_hits.astype(F32),
        (((1,), (1,)), ((), ())),
        precision=HIGHEST,
        preferred_element_type=F32,
    ).reshape(-1)

    vector_grads = (
        mask_vector_grad,
        gain_one_grad,
        shift_one_grad,
        qkv_bias_grad[:, 0].reshape(D),
        qkv_bias_grad[:, 2].reshape(D),
        mix_bias_grad,
        gain_two_grad,
        shift_two_grad,
        final_bias_grad,
        table_grad,
        inner_bias_grad,
        contrast_bias_grad,
        codebook_grad,
    )
    columns = []
    for grad, v, w in zip(vector_grads, vectors, widths):
        by_device = grad.reshape(grid.total, v.shape[0])
        by_device = jnp.pad(by_device, ((0, 0), (0, shard * w - v.shape[0])))
        columns.append(by_device.reshape(grid.total * shard, w).astype(BF16))
    fill = jnp.zeros((D, small_width - CD - CODES - sum(widths)), BF16)
    last = jnp.concatenate(
        [qkv_map_grad, mix_map_grad, contrast_map_grad.astype(BF16), score_map_grad.astype(BF16)]
        + columns
        + [fill],
        axis=1,
    )
    last = scatter_rows(grid, last)
    qkv_shard = last[:, : 3 * D].reshape(shard, PAIRS, 3, 128)
    query_shard, key_shard, value_shard = [qkv_shard[:, :, i].reshape(shard, D) for i in range(3)]
    at = 3 * D
    mix_shard, at = last[:, at : at + D], at + D
    contrast_shard, at = last[:, at : at + CD], at + CD
    score_shard, at = last[:, at : at + CODES], at + CODES
    flats = []
    for v, w in zip(vectors, widths):
        flats.append(last[:, at : at + w].reshape(-1)[: v.shape[0]])
        at += w
    (
        mask_out,
        gain_one_out,
        shift_one_out,
        query_bias_out,
        value_bias_out,
        mix_bias_out,
        gain_two_out,
        shift_two_out,
        final_bias_out,
        table_out,
        inner_bias_out,
        contrast_bias_out,
        codebook_out,
    ) = flats
    return (
        encoded_out,
        frames_grad,
        mask_out,
        gain_one_out,
        shift_one_out,
        query_shard,
        query_bias_out,
        key_shard,
        value_shard,
        value_bias_out,
        mix_shard,
        mix_bias_out,
        table_out,
        gain_two_out,
        shift_two_out,
        entry_shard,
        inner_bias_out,
        final_shard,
        final_bias_out,
        score_shard,
        codebook_out,
        contrast_shard,
        contrast_bias_out,
    )


def solution(mesh):
    both = ("dp", "seq")
    split, lines, flat = P("dp", "seq", None), P(both, None), P(both)
    placed = (
        (split, split, split, P(), P("dp"), P("dp", None), P("dp", None), P())
        + (flat, flat, flat, lines, flat, lines, lines, flat, lines, flat, flat)
        + (flat, flat, lines, flat, lines, flat)
        + (lines, flat, lines, flat)
    )
    results = (
        (split, split, flat, flat, flat, lines, flat, lines, lines, flat, lines, flat, flat)
        + (flat, flat, lines, flat, lines, flat)
        + (lines, flat, lines, flat)
    )
    return jax.shard_map(
        functools.partial(body, Grid(mesh)),
        mesh=mesh,
        in_specs=placed,
        out_specs=results,
        check_vma=False,
    )
```

time: 2500 us -> 611 us (0.24)
  waiting for transfers between devices: 957 us -> 168 us
  other arithmetic: 420 us -> 38.8 us
  local copies, waits for them, and re-layouts: 445 us -> 116 us
  matrix products: 363 us -> 99.6 us
  blocking collectives: 258 us -> 0 us
  starting transfers between devices: 1.3 us -> 121 us
  Pallas kernels: 0 us -> 53.4 us
    reduce_scatter x8 -> x0, waiting for transfers between devices: 576 us -> none  [the longest x1 142 us: body(): lax.psum_scatter(inner_weight_grad, ('dp', 'seq'), scatter_dimension=0, t...]
    scatter-add x1 -> x0, other arithmetic: 348 us -> none  [local_bias(): return per_offset[:, offsets]]
    unnamed x27 -> x0, waiting for transfers between devices: 279 us -> none
    dot_general x73 -> x23, matrix products: 363 us -> 99.6 us  [the longest x7 38.5 us: dot_nt(): lax.dot_general(a, b, (((1,), (1,)), ((), ())), preferred_element_type=F32)]
    gather x2 -> x0, local copies, waits for them, and re-layouts: 257 us -> none  [local_bias(): return per_offset[:, offsets]]
    all_gather x2 -> x0, blocking collectives: 215 us -> none  [the longest x1 144 us: head_weights(): lax.all_gather(contrast_space_map, ('dp', 'seq'), axis=0, tiled=True)]
    ppermute x0 -> x67, waiting for transfers between devices: none -> 168 us  [swap(): return lax.ppermute(value, axis, pairs)]
    ppermute x0 -> x67, starting transfers between devices: none -> 121 us  [swap(): return lax.ppermute(value, axis, pairs)]
  transfers between devices with their start and end apart: 22 -> 67, of which waited for: 10 -> 22; matrix products, arithmetic and copies ran while one was open for 48% -> 24% of each run, Pallas kernels for 0% -> 9%
where the time goes in v1:
time: 611 us; the launch traced here: 600 us
  waiting for transfers between devices  168 us (27%)
  starting transfers between devices  121 us (20%)
  local copies, waits for them, and re-layouts  116 us (19%)
  matrix products  99.6 us (16%)
  Pallas kernels  53.4 us (9%)
  other arithmetic  38.8 us (6%)
    ppermute x67, waiting for transfers between devices, swap(): return lax.ppermute(value, axis, pairs)  168 us
    ppermute x67, starting transfers between devices, swap(): return lax.ppermute(value, axis, pairs)  121 us
    dot_general x7, matrix products, dot_nt(): lax.dot_general(a, b, (((1,), (1,)), ((), ())), preferred_element_type=F32)  38.5 us
    pallas_call x1, Pallas kernels, attend_back(): pl.pallas_call(functools.partial(attend_back_kernel, own), grid=(PAIRS, o...  32.6 us
    dot_general x7, matrix products, dot_tn(): lax.dot_general(a, b, (((0,), (0,)), ((), ())), preferred_element_type=F32)  30.2 us
    dot_general x8, matrix products, dot_nn(): lax.dot_general(a, b, (((1,), (0,)), ((), ())), preferred_element_type=F32)  30.2 us
    dynamic_update_slice x39, local copies, waits for them, and re-layouts, gather_rows(): out = lax.dynamic_update_slice_in_dim(out, part, me ^ d, axis=j)  23 us
    pallas_call x1, Pallas kernels, attend(): pl.pallas_call(attend_kernel, grid=(PAIRS, own), in_specs=[pl.BlockSpec((...  18.4 us
  transfers between devices with their start and end apart: 67, of which 22 were waited for; matrix products, arithmetic and copies ran while one was open for 24% of the time, Pallas kernels for 9%

profile of v1, /device:TPU:0, one launch (start us, length us, event | category | flops | bytes accessed | tf_op | source)
XLA Modules:
  0.0 599.9 jit_solution(3696811518338145223)
XLA Ops:
  12.0 3.0 collective-permute-start
  19.6 3.5 collective-permute-start.18
  43.6 3.8 collective-permute-start.11
  49.5 2.9 collective-permute-start.12
  53.0 5.7 collective-permute-done.11
  65.5 3.1 collective-permute-done.4
  71.1 3.0 collective-permute-done.5
  74.1 2.8 collective-permute-start.25
  81.2 3.2 collective-permute-start.7
  87.0 5.3 collective-permute-start.8
  97.1 3.9 collective-permute-start.35
  103.4 3.1 collective-permute-start.36
  106.5 12.8 %collective-permute-done.8 = bf16[2,128,768]{2,1,0:T(8,128)(2,1)S(1)} collective-permute-done((bf16[2,128,768]{2,1,0:T(8,128)(2,1)S(1)}, bf16[2,128,768]{2,1,0:T(8,128)(2,1)S(1)}, u32[]{:S(2)}, u32[]{:S(2)}) %collective-permute-start.8) | collective-permute-done | bytes 393248 | tf_op jit(solution)/shard_map/ppermute | solution.py:254
  123.8 24.0 %collective-permute-done.35 = bf16[2,128,768]{2,1,0:T(8,128)(2,1)S(1)} collective-permute-done((bf16[2,128,768]{2,1,0:T(8,128)(2,1)S(1)}, bf16[2,128,768]{2,1,0:T(8,128)(2,1)S(1)}, u32[]{:S(2)}, u32[]{:S(2)}) %collective-permute-start.35) | collective-permute-done | bytes 393248 | tf_op jit(solution)/shard_map/ppermute | solution.py:254
  179.1 4.5 collective-permute-start.37
  189.1 7.5 %collective-permute-done.38 = bf16[2,128,256]{2,1,0:T(8,128)(2,1)S(1)} collective-permute-done((bf16[2,128,256]{2,1,0:T(8,128)(2,1)S(1)}, bf16[2,128,256]{2,1,0:T(8,128)(2,1)S(1)}, u32[]{:S(2)}, u32[]{:S(2)}) %collective-permute-start.38) | collective-permute-done | bytes 131104 | tf_op jit(solution)/shard_map/ppermute | solution.py:254
  197.8 5.6 collective-permute-done.39
  209.4 2.9 copy-done.2
  212.3 17.9 %collective-permute-done.21 = bf16[1,1,4,24,3840]{4,3,2,1,0:T(8,128)(2,1)S(1)} collective-permute-done((bf16[1,1,4,24,3840]{4,3,2,1,0:T(8,128)(2,1)S(1)}, bf16[1,1,4,24,3840]{4,3,2,1,0:T(8,128)(2,1)S(1)}, u32[]{:S(2)}, u32[]{:S(2)}) %collective-permute-start.21) | collective-permute-done | bytes 737312 | tf_op jit(solution)/shard_map/ppermute | solution.py:254
  232.0 4.1 add_convert_fusion.qkv_ref
  236.1 18.4 %attend.1 = (bf16[1024,768]{1,0:T(8,128)(2,1)S(1)}, f32[6,2,2,512]{3,2,1,0:T(2,128)S(1)}) custom-call(bf16[1024,2304]{1,0:T(8,128)(2,1)S(1)} %add_convert_fusion.qkv_ref, f32[1024,1]{1,0:T(8,128)S(1)} %bitcast.242, f32[6,2,1024]{2,1,0:T(2,128)S(1)} %copy.142.w_ref), custom_call_target="tpu_custom_call" | custom-call | flops 19327352832 | bytes 10000000 | tf_op jit(solution)/shard_map/attend/pallas_call | solution.py:83
  260.7 9.9 %multiply_convert_fusion.1 = (bf16[1024,3072]{1,0:T(8,128)(2,1)}, f32[1024,3072]{1,0:T(8,128)}) fusion(f32[3072]{0:T(1024)S(1)} %copy-done.69, bf16[768,3840]{1,0:T(8,128)(2,1)S(1)} %bitcast.268, f32[1024,768]{1,0:T(8,128)S(1)} %get-tuple-element.126, f32[768]{0:T(1024)S(1)} %copy-done.72, f32[768]{0:T(1024)S(1)} %copy-done.66, ...), kind=kOutput, calls=%fused_computation.7 | convolution fusion | flops 4854644736 | bytes 26767360 | tf_op jit(solution)/shard_map/dot_general | solution.py:37
  270.6 9.0 %add_convert_fusion.5 = bf16[1024,768]{1,0:T(8,128)(2,1)S(1)} fusion(f32[1024,768]{1,0:T(8,128)S(1)} %get-tuple-element.126, bf16[1024,3072]{1,0:T(8,128)(2,1)} %get-tuple-element.127, bf16[3072,768]{1,0:T(8,128)(2,1)} %bitcast.281, f32[768]{0:T(1024)S(1)} %copy-done.73), kind=kOutput, calls=%fused_computation.33 | convolution fusion | flops 4834197504 | bytes 15731712 | tf_op jit(solution)/shard_map/dot_general | solution.py:37
  286.2 9.8 %convolution_convert_fusion = bf16[3072,768]{1,0:T(8,128)(2,1)} fusion(bf16[1024,3072]{1,0:T(8,128)(2,1)} %get-tuple-element.127, bf16[1024,768]{1,0:T(8,128)(2,1)S(1)} %get-tuple-element.73), kind=kOutput, calls=%fused_computation.11 | convolution fusion | flops 4834197504 | bytes 12582912 | tf_op jit(solution)/shard_map/dot_general | solution.py:41
  296.1 13.4 %fusion.62 = (bf16[3072]{0:T(1024)(128)(2,1)S(1)}, bf16[1024,3072]{1,0:T(8,128)(2,1)}) fusion(f32[1024,3072]{1,0:T(8,128)} %get-tuple-element.128, f32[3072]{0:T(1024)S(1)} %copy-done.69, bf16[1024,768]{1,0:T(8,128)(2,1)S(1)} %get-tuple-element.73, bf16[3072,768]{1,0:T(8,128)(2,1)S(1)} %bitcast.284), kind=kOutput, calls=%fused_computation.283 | convolution fusion | flops 4875875328 | bytes 25184256 | tf_op jit(solution)/shard_map/dot_general | solution.py:33
  309.5 10.0 %convolution_convert_fusion.1 = bf16[768,3072]{1,0:T(8,128)(2,1)} fusion(bf16[1024,3072]{1,0:T(8,128)(2,1)} %get-tuple-element.137, f32[1024,768]{1,0:T(8,128)S(1)} %get-tuple-element.126, f32[768]{0:T(1024)S(1)} %copy-done.72, f32[768]{0:T(1024)S(1)} %copy-done.66, f32[1024]{0:T(1024)S(1)} %add_rsqrt_fusion.1, f32[1024]{0:T(1024)S(1)} %broadcast_multiply_fusion.4), kind=kOutput, calls=%fused_computation.12 | convolution fusion | flops 4838129664 | bytes 14170112 | tf_op jit(solution)/shard_map/dot_general | solution.py:41
  319.5 9.5 %multiply_reduce_fusion = (bf16[768]{0:T(1024)(128)(2,1)S(1)}, f32[1024]{0:T(1024)S(1)}, f32[1024]{0:T(1024)S(1)}, bf16[768]{0:T(1024)(128)(2,1)S(1)}, f32[1024,768]{1,0:T(8,128)S(1)}) fusion(f32[1024,768]{1,0:T(8,128)S(1)} %get-tuple-element.126, f32[1024]{0:T(1024)S(1)} %add_rsqrt_fusion.1, f32[1024]{0:T(1024)S(1)} %broadcast_multiply_fusion.4, ...), kind=kOutput, calls=%fused_computation.23 | convolution fusion | flops 4838912000 | bytes 17324032 | tf_op jit(solution)/shard_map/dot_general | solution.py:33
  329.0 2.7 convert_reduce_fusion.9
  334.3 3.1 convolution_convert_fusion.3.grad_ref
  346.4 32.6 %attend_back.1 = (bf16[1024,2304]{1,0:T(8,128)(2,1)S(1)}, f32[6,2,1024]{2,1,0:T(2,128)S(1)}) custom-call(bf16[1024,2304]{1,0:T(8,128)(2,1)S(1)} %add_convert_fusion.qkv_ref, bf16[1024,768]{1,0:T(8,128)(2,1)S(1)} %convolution_convert_fusion.3.grad_ref, f32[6,2,2,512]{3,2,1,0:T(2,128)S(1)} %get-tuple-element.31.total_ref, f32[1024,1]{1,0:T(8,128)S(1)} %bitcast.243, ...), custom_call_target="tpu_custom_call" | custom-call | flops 32212254720 | bytes 14000000 | tf_op jit(solution)/shard_map/attend_back/pallas_call | solution.py:160
  379.1 8.3 %multiply_reduce_fusion.1 = (bf16[768]{0:T(1024)(128)(2,1)S(1)}, f32[1024]{0:T(1024)S(1)}, f32[1024]{0:T(1024)S(1)}, bf16[768]{0:T(1024)(128)(2,1)S(1)}, f32[1024,768]{1,0:T(8,128)S(1)}) fusion(bf16[2,4,128,768]{3,2,1,0:T(8,128)(2,1)S(1)} %bitcast_dynamic-update-slice_fusion.12, f32[1024]{0:T(1024)S(1)} %bitcast.308, f32[1024]{0:T(1024)S(1)} %bitcast.306, ...), kind=kOutput, calls=%fused_computation.24 | convolution fusion | flops 3632525824 | bytes 13002752 | tf_op jit(solution)/shard_map/dot_general | solution.py:33
  387.4 2.8 select_reduce_fusion
  390.2 5.6 convolution_convert_fusion.2
  396.5 3.1 reduce.6
  435.3 10.8 %concatenate.28 = bf16[4,2,4,24,3584]{4,3,2,1,0:T(8,128)(2,1)} concatenate(bf16[4,2,4,24,2304]{4,3,2,1,0:T(8,128)(2,1)} %bitcast.287, bf16[4,2,4,24,768]{4,3,2,1,0:T(8,128)(2,1)S(1)} %bitcast.295, bf16[4,2,4,24,256]{4,3,2,1,0:T(8,128)(2,1)} %bitcast.299, bf16[4,2,4,24,200]{4,3,2,1,0:T(8,128)(2,1)S(1)} %bitcast.294, bf16[4,2,4,24,1]{4,3,2,1,0:T(8,128)(2,1)} %convert_element_type.588, ...), dimensions={4} | concatenate | bytes 11010048 | tf_op jit(solution)/shard_map/concatenate | solution.py:609
  456.6 4.5 collective-permute-done.31
  461.1 22.5 %collective-permute-done.32 = bf16[2,128,768]{2,1,0:T(8,128)(2,1)S(1)} collective-permute-done((bf16[2,128,768]{2,1,0:T(8,128)(2,1)S(1)}, bf16[2,128,768]{2,1,0:T(8,128)(2,1)S(1)}, u32[]{:S(2)}, u32[]{:S(2)}) %collective-permute-start.32) | collective-permute-done | bytes 393248 | tf_op jit(solution)/shard_map/ppermute | solution.py:254
  485.9 3.2 add_convert_fusion.2
  498.5 19.7 %collective-permute-done.54 = bf16[1,1,4,24,3072]{4,3,2,1,0:T(8,128)(2,1)S(1)} collective-permute-done((bf16[1,1,4,24,3072]{4,3,2,1,0:T(8,128)(2,1)S(1)}, bf16[1,1,4,24,3072]{4,3,2,1,0:T(8,128)(2,1)S(1)}, u32[]{:S(2)}, u32[]{:S(2)}) %collective-permute-start.54) | collective-permute-done | bytes 589856 | tf_op jit(solution)/shard_map/ppermute | solution.py:254
  519.7 14.9 %collective-permute-done.55 = bf16[1,1,4,24,3072]{4,3,2,1,0:T(8,128)(2,1)S(1)} collective-permute-done((bf16[1,1,4,24,3072]{4,3,2,1,0:T(8,128)(2,1)S(1)}, bf16[1,1,4,24,3072]{4,3,2,1,0:T(8,128)(2,1)S(1)}, u32[]{:S(2)}, u32[]{:S(2)}) %collective-permute-start.55) | collective-permute-done | bytes 589856 | tf_op jit(solution)/shard_map/ppermute | solution.py:254
  534.6 4.3 collective-permute-start.47
  538.8 3.0 collective-permute-start.48
  542.3 10.6 %collective-permute-start.57 = (bf16[1,1,1,24,3072]{4,3,2,1,0:T(8,128)(2,1)S(1)}, bf16[1,1,1,24,3072]{4,3,2,1,0:T(8,128)(2,1)S(1)}, u32[]{:S(2)}, u32[]{:S(2)}) collective-permute-start(bf16[1,1,1,24,3072]{4,3,2,1,0:T(8,128)(2,1)S(1)} %get-tuple-element.110), channel_id=1, source_target_pairs={{0,1},{1,0},{2,3},{3,2},{4,5},{5,4},{6,7},{7,6},{8,9},{9,8},{10,11... | collective-permute-start | bytes 442376 | tf_op jit(solution)/shard_map/ppermute | solution.py:254
  557.0 6.7 %collective-permute-done.58 = bf16[1,1,1,24,3072]{4,3,2,1,0:T(8,128)(2,1)S(1)} collective-permute-done((bf16[1,1,1,24,3072]{4,3,2,1,0:T(8,128)(2,1)S(1)}, bf16[1,1,1,24,3072]{4,3,2,1,0:T(8,128)(2,1)S(1)}, u32[]{:S(2)}, u32[]{:S(2)}) %collective-permute-start.58) | collective-permute-done | bytes 147488 | tf_op jit(solution)/shard_map/ppermute | solution.py:254
  563.6 3.8 collective-permute-start.65
  570.5 8.7 %collective-permute-start.50 = (bf16[1,1,1,24,3584]{4,3,2,1,0:T(8,128)(2,1)S(1)}, bf16[1,1,1,24,3584]{4,3,2,1,0:T(8,128)(2,1)S(1)}, u32[]{:S(2)}, u32[]{:S(2)}) collective-permute-start(bf16[1,1,1,24,3584]{4,3,2,1,0:T(8,128)(2,1)S(1)} %get-tuple-element.104), channel_id=1, source_target_pairs={{0,1},{1,0},{2,3},{3,2},{4,5},{5,4},{6,7},{7,6},{8,9},{9,8},{10,11... | collective-permute-start | bytes 516104 | tf_op jit(solution)/shard_map/ppermute | solution.py:254
  582.5 3.3 collective-permute-done.50
  585.8 5.3 collective-permute-done.51
  (533 shorter events, 214.1 us)
Async XLA Ops:
  12.0 29.5 %collective-permute-start = (bf16[1,1,1,24,512]{4,3,2,1,0:T(8,128)(2,1)}, bf16[1,1,1,24,512]{4,3,2,1,0:T(8,128)(2,1)}, u32[]{:S(2)}, u32[]{:S(2)}) collective-permute-start(bf16[1,1,1,24,512]{4,3,2,1,0:T(8,128)(2,1)} %bitcast.10), channel_id=1, source_target_pairs={{0,1},{1,0},{2,3},{3,2},{4,5},{5,4},{6,7},{7,6},{8,9},{9,8},{10,11... | collective-permute-start | bytes 73736 | tf_op jit(solution)/shard_map/ppermute | solution.py:254
  15.1 27.3 %collective-permute-start.1 = (bf16[1,1,1,24,512]{4,3,2,1,0:T(8,128)(2,1)}, bf16[1,1,1,24,512]{4,3,2,1,0:T(8,128)(2,1)}, u32[]{:S(2)}, u32[]{:S(2)}) collective-permute-start(bf16[1,1,1,24,512]{4,3,2,1,0:T(8,128)(2,1)} %bitcast.10), channel_id=1, source_target_pairs={{0,2},{1,3},{2,0},{3,1},{4,6},{5,7},{6,4},{7,5},{8,10},{9,11},{10,... | collective-permute-start | bytes 73736 | tf_op jit(solution)/shard_map/ppermute | solution.py:254
  17.7 26.0 %collective-permute-start.2 = (bf16[1,1,1,24,512]{4,3,2,1,0:T(8,128)(2,1)}, bf16[1,1,1,24,512]{4,3,2,1,0:T(8,128)(2,1)}, u32[]{:S(2)}, u32[]{:S(2)}) collective-permute-start(bf16[1,1,1,24,512]{4,3,2,1,0:T(8,128)(2,1)} %bitcast.10), channel_id=1, source_target_pairs={{0,3},{1,2},{2,1},{3,0},{4,7},{5,6},{6,5},{7,4},{8,11},{9,10},{10,... | collective-permute-start | bytes 73736 | tf_op jit(solution)/shard_map/ppermute | solution.py:254
  18.6 75.8 %collective-permute-start.17 = (bf16[1,1,1,24,3840]{4,3,2,1,0:T(8,128)(2,1)S(1)}, bf16[1,1,1,24,3840]{4,3,2,1,0:T(8,128)(2,1)}, u32[]{:S(2)}, u32[]{:S(2)}) collective-permute-start(bf16[1,1,1,24,3840]{4,3,2,1,0:T(8,128)(2,1)S(1)} %maximum_bitcast_fusion), channel_id=1, source_target_pairs={{0,1},{1,0},{2,3},{3,2},{4,5},{5,4},{6,7},{7,6},{8,9},{9,8},{10,11... | collective-permute-start | bytes 552968 | tf_op jit(solution)/shard_map/ppermute | solution.py:254
  19.6 76.1 %collective-permute-start.18 = (bf16[1,1,1,24,3840]{4,3,2,1,0:T(8,128)(2,1)S(1)}, bf16[1,1,1,24,3840]{4,3,2,1,0:T(8,128)(2,1)}, u32[]{:S(2)}, u32[]{:S(2)}) collective-permute-start(bf16[1,1,1,24,3840]{4,3,2,1,0:T(8,128)(2,1)S(1)} %maximum_bitcast_fusion), channel_id=1, source_target_pairs={{0,2},{1,3},{2,0},{3,1},{4,6},{5,7},{6,4},{7,5},{8,10},{9,11},{10,... | collective-permute-start | bytes 552968 | tf_op jit(solution)/shard_map/ppermute | solution.py:254
  41.6 55.5 %collective-permute-start.19 = (bf16[1,1,1,24,3840]{4,3,2,1,0:T(8,128)(2,1)S(1)}, bf16[1,1,1,24,3840]{4,3,2,1,0:T(8,128)(2,1)S(1)}, u32[]{:S(2)}, u32[]{:S(2)}) collective-permute-start(bf16[1,1,1,24,3840]{4,3,2,1,0:T(8,128)(2,1)S(1)} %maximum_bitcast_fusion), channel_id=1, source_target_pairs={{0,3},{1,2},{2,1},{3,0},{4,7},{5,6},{6,5},{7,4},{8,11},{9,10},{10,... | collective-permute-start | bytes 552968 | tf_op jit(solution)/shard_map/ppermute | solution.py:254
  43.6 15.1 %collective-permute-start.11 = (bf16[1,1,1,24,2304]{4,3,2,1,0:T(8,128)(2,1)S(1)}, bf16[1,1,1,24,2304]{4,3,2,1,0:T(8,128)(2,1)S(1)}, u32[]{:S(2)}, u32[]{:S(2)}) collective-permute-start(bf16[1,1,1,24,2304]{4,3,2,1,0:T(8,128)(2,1)S(1)} %reshape_reshape.28), channel_id=1, source_target_pairs={{0,2},{1,3},{2,0},{3,1},{4,6},{5,7},{6,4},{7,5},{8,10},{9,11},{10,... | collective-permute-start | bytes 331784 | tf_op jit(solution)/shard_map/ppermute | solution.py:254
  58.7 18.3 %collective-permute-start.24 = (bf16[1,1,1,96,768]{4,3,2,1,0:T(8,128)(2,1)}, bf16[1,1,1,96,768]{4,3,2,1,0:T(8,128)(2,1)S(1)}, u32[]{:S(2)}, u32[]{:S(2)}) collective-permute-start(bf16[1,1,1,96,768]{4,3,2,1,0:T(8,128)(2,1)} %bitcast.300), channel_id=1, source_target_pairs={{0,1},{1,0},{2,3},{3,2},{4,5},{5,4},{6,7},{7,6},{8,9},{9,8},{10,11... | collective-permute-start | bytes 442376 | tf_op jit(solution)/shard_map/ppermute | solution.py:254
  81.2 22.2 %collective-permute-start.7 = (bf16[2,128,768]{2,1,0:T(8,128)(2,1)S(1)}, bf16[2,128,768]{2,1,0:T(8,128)(2,1)S(1)}, u32[]{:S(2)}, u32[]{:S(2)}) collective-permute-start(bf16[2,128,768]{2,1,0:T(8,128)(2,1)S(1)} %copy-done.38), channel_id=1, source_target_pairs={{0,1},{1,0},{2,3},{3,2},{4,5},{5,4},{6,7},{7,6},{8,9},{9,8},{10,11... | collective-permute-start | bytes 1179656 | tf_op jit(solution)/shard_map/ppermute | solution.py:254
  87.0 32.3 %collective-permute-start.8 = (bf16[2,128,768]{2,1,0:T(8,128)(2,1)S(1)}, bf16[2,128,768]{2,1,0:T(8,128)(2,1)S(1)}, u32[]{:S(2)}, u32[]{:S(2)}) collective-permute-start(bf16[2,128,768]{2,1,0:T(8,128)(2,1)S(1)} %copy-done.37), channel_id=1, source_target_pairs={{0,2},{1,3},{2,0},{3,1},{4,6},{5,7},{6,4},{7,5},{8,10},{9,11},{10,... | collective-permute-start | bytes 1179656 | tf_op jit(solution)/shard_map/ppermute | solution.py:254
  94.4 26.4 %collective-permute-start.9 = (bf16[2,128,768]{2,1,0:T(8,128)(2,1)S(1)}, bf16[2,128,768]{2,1,0:T(8,128)(2,1)S(1)}, u32[]{:S(2)}, u32[]{:S(2)}) collective-permute-start(bf16[2,128,768]{2,1,0:T(8,128)(2,1)S(1)} %copy-done.36), channel_id=1, source_target_pairs={{0,3},{1,2},{2,1},{3,0},{4,7},{5,6},{6,5},{7,4},{8,11},{9,10},{10,... | collective-permute-start | bytes 1179656 | tf_op jit(solution)/shard_map/ppermute | solution.py:254
  95.7 26.8 %collective-permute-start.34 = (bf16[2,128,768]{2,1,0:T(8,128)(2,1)S(1)}, bf16[2,128,768]{2,1,0:T(8,128)(2,1)S(1)}, u32[]{:S(2)}, u32[]{:S(2)}) collective-permute-start(bf16[2,128,768]{2,1,0:T(8,128)(2,1)S(1)} %copy-done.35), channel_id=1, source_target_pairs={{0,1},{1,0},{2,3},{3,2},{4,5},{5,4},{6,7},{7,6},{8,9},{9,8},{10,11... | collective-permute-start | bytes 1179656 | tf_op jit(solution)/shard_map/ppermute | solution.py:254
  97.1 50.8 %collective-permute-start.35 = (bf16[2,128,768]{2,1,0:T(8,128)(2,1)S(1)}, bf16[2,128,768]{2,1,0:T(8,128)(2,1)S(1)}, u32[]{:S(2)}, u32[]{:S(2)}) collective-permute-start(bf16[2,128,768]{2,1,0:T(8,128)(2,1)S(1)} %copy-done.34), channel_id=1, source_target_pairs={{0,2},{1,3},{2,0},{3,1},{4,6},{5,7},{6,4},{7,5},{8,10},{9,11},{10,... | collective-permute-start | bytes 1179656 | tf_op jit(solution)/shard_map/ppermute | solution.py:254
  103.4 45.2 %collective-permute-start.36 = (bf16[2,128,768]{2,1,0:T(8,128)(2,1)S(1)}, bf16[2,128,768]{2,1,0:T(8,128)(2,1)S(1)}, u32[]{:S(2)}, u32[]{:S(2)}) collective-permute-start(bf16[2,128,768]{2,1,0:T(8,128)(2,1)S(1)} %get-tuple-element.95), channel_id=1, source_target_pairs={{0,3},{1,2},{2,1},{3,0},{4,7},{5,6},{6,5},{7,4},{8,11},{9,10},{10,... | collective-permute-start | bytes 1179656 | tf_op jit(solution)/shard_map/ppermute | solution.py:254
  119.3 55.6 %collective-permute-start.13 = (bf16[1,1,4,24,2304]{4,3,2,1,0:T(8,128)(2,1)}, bf16[1,1,4,24,2304]{4,3,2,1,0:T(8,128)(2,1)}, u32[]{:S(2)}, u32[]{:S(2)}) collective-permute-start(bf16[1,1,4,24,2304]{4,3,2,1,0:T(8,128)(2,1)} %constant_dynamic-update-slice_fusion.26), channel_id=1, source_target_pairs={{0,8},{4,12},{8,0},{12,4},{16,24},{20,28},{24,16},{28,20},{1,9},{5... | collective-permute-start | bytes 1327112 | tf_op jit(solution)/shard_map/ppermute | solution.py:254
  120.9 55.6 %collective-permute-start.14 = (bf16[1,1,4,24,2304]{4,3,2,1,0:T(8,128)(2,1)}, bf16[1,1,4,24,2304]{4,3,2,1,0:T(8,128)(2,1)}, u32[]{:S(2)}, u32[]{:S(2)}) collective-permute-start(bf16[1,1,4,24,2304]{4,3,2,1,0:T(8,128)(2,1)} %constant_dynamic-update-slice_fusion.26), channel_id=1, source_target_pairs={{0,16},{4,20},{8,24},{12,28},{16,0},{20,4},{24,8},{28,12},{1,17},{... | collective-permute-start | bytes 1327112 | tf_op jit(solution)/shard_map/ppermute | solution.py:254
  122.5 56.6 %collective-permute-start.15 = (bf16[1,1,4,24,2304]{4,3,2,1,0:T(8,128)(2,1)}, bf16[1,1,4,24,2304]{4,3,2,1,0:T(8,128)(2,1)}, u32[]{:S(2)}, u32[]{:S(2)}) collective-permute-start(bf16[1,1,4,24,2304]{4,3,2,1,0:T(8,128)(2,1)} %constant_dynamic-update-slice_fusion.26), channel_id=1, source_target_pairs={{0,24},{4,28},{8,16},{12,20},{16,8},{20,12},{24,0},{28,4},{1,25},{... | collective-permute-start | bytes 1327112 | tf_op jit(solution)/shard_map/ppermute | solution.py:254
  148.6 56.4 %collective-permute-start.27 = (bf16[1,1,4,96,768]{4,3,2,1,0:T(8,128)(2,1)}, bf16[1,1,4,96,768]{4,3,2,1,0:T(8,128)(2,1)}, u32[]{:S(2)}, u32[]{:S(2)}) collective-permute-start(bf16[1,1,4,96,768]{4,3,2,1,0:T(8,128)(2,1)} %constant_dynamic-update-slice_fusion.6), channel_id=1, source_target_pairs={{0,8},{4,12},{8,0},{12,4},{16,24},{20,28},{24,16},{28,20},{1,9},{5... | collective-permute-start | bytes 1769480 | tf_op jit(solution)/shard_map/ppermute | solution.py:254
  150.9 55.8 %collective-permute-start.28 = (bf16[1,1,4,96,768]{4,3,2,1,0:T(8,128)(2,1)}, bf16[1,1,4,96,768]{4,3,2,1,0:T(8,128)(2,1)}, u32[]{:S(2)}, u32[]{:S(2)}) collective-permute-start(bf16[1,1,4,96,768]{4,3,2,1,0:T(8,128)(2,1)} %constant_dynamic-update-slice_fusion.6), channel_id=1, source_target_pairs={{0,16},{4,20},{8,24},{12,28},{16,0},{20,4},{24,8},{28,12},{1,17},{... | collective-permute-start | bytes 1769480 | tf_op jit(solution)/shard_map/ppermute | solution.py:254
  174.9 33.0 %collective-permute-start.29 = (bf16[1,1,4,96,768]{4,3,2,1,0:T(8,128)(2,1)}, bf16[1,1,4,96,768]{4,3,2,1,0:T(8,128)(2,1)S(1)}, u32[]{:S(2)}, u32[]{:S(2)}) collective-permute-start(bf16[1,1,4,96,768]{4,3,2,1,0:T(8,128)(2,1)} %constant_dynamic-update-slice_fusion.6), channel_id=1, source_target_pairs={{0,24},{4,28},{8,16},{12,20},{16,8},{20,12},{24,0},{28,4},{1,25},{... | collective-permute-start | bytes 1769480 | tf_op jit(solution)/shard_map/ppermute | solution.py:254
  176.5 32.8 %collective-permute-start.20 = (bf16[1,1,4,24,3840]{4,3,2,1,0:T(8,128)(2,1)S(1)}, bf16[1,1,4,24,3840]{4,3,2,1,0:T(8,128)(2,1)S(1)}, u32[]{:S(2)}, u32[]{:S(2)}) collective-permute-start(bf16[1,1,4,24,3840]{4,3,2,1,0:T(8,128)(2,1)S(1)} %copy-done.27), channel_id=1, source_target_pairs={{0,8},{4,12},{8,0},{12,4},{16,24},{20,28},{24,16},{28,20},{1,9},{5... | collective-permute-start | bytes 2211848 | tf_op jit(solution)/shard_map/ppermute | solution.py:254
  203.5 26.8 %collective-permute-start.21 = (bf16[1,1,4,24,3840]{4,3,2,1,0:T(8,128)(2,1)S(1)}, bf16[1,1,4,24,3840]{4,3,2,1,0:T(8,128)(2,1)S(1)}, u32[]{:S(2)}, u32[]{:S(2)}) collective-permute-start(bf16[1,1,4,24,3840]{4,3,2,1,0:T(8,128)(2,1)S(1)} %copy-done.27), channel_id=1, source_target_pairs={{0,16},{4,20},{8,24},{12,28},{16,0},{20,4},{24,8},{28,12},{1,17},{... | collective-permute-start | bytes 2211848 | tf_op jit(solution)/shard_map/ppermute | solution.py:254
  205.0 25.3 %collective-permute-start.22 = (bf16[1,1,4,24,3840]{4,3,2,1,0:T(8,128)(2,1)S(1)}, bf16[1,1,4,24,3840]{4,3,2,1,0:T(8,128)(2,1)S(1)}, u32[]{:S(2)}, u32[]{:S(2)}) collective-permute-start(bf16[1,1,4,24,3840]{4,3,2,1,0:T(8,128)(2,1)S(1)} %copy-done.27), channel_id=1, source_target_pairs={{0,24},{4,28},{8,16},{12,20},{16,8},{20,12},{24,0},{28,4},{1,25},{... | collective-permute-start | bytes 2211848 | tf_op jit(solution)/shard_map/ppermute | solution.py:254
  206.7 24.6 %collective-permute-start.16 = (bf16[4,1,4,24,2304]{4,3,2,1,0:T(8,128)(2,1)S(1)}, bf16[4,1,4,24,2304]{4,3,2,1,0:T(8,128)(2,1)S(1)}, u32[]{:S(2)}, u32[]{:S(2)}) collective-permute-start(bf16[4,1,4,24,2304]{4,3,2,1,0:T(8,128)(2,1)S(1)} %constant_dynamic-update-slice_fusion.22), channel_id=1, source_target_pairs={{0,4},{4,0},{8,12},{12,8},{16,20},{20,16},{24,28},{28,24},{1,5},{5... | collective-permute-start | bytes 5308424 | tf_op jit(solution)/shard_map/ppermute | solution.py:254
  207.9 46.5 %collective-permute-start.30 = (bf16[4,1,4,96,768]{4,3,2,1,0:T(8,128)(2,1)S(1)}, bf16[4,1,4,96,768]{4,3,2,1,0:T(8,128)(2,1)S(1)}, u32[]{:S(2)}, u32[]{:S(2)}) collective-permute-start(bf16[4,1,4,96,768]{4,3,2,1,0:T(8,128)(2,1)S(1)} %constant_dynamic-update-slice_fusion.2), channel_id=1, source_target_pairs={{0,4},{4,0},{8,12},{12,8},{16,20},{20,16},{24,28},{28,24},{1,5},{5... | collective-permute-start | bytes 7077896 | tf_op jit(solution)/shard_map/ppermute | solution.py:254
  230.4 25.6 %collective-permute-start.23 = (bf16[4,1,4,24,3840]{4,3,2,1,0:T(8,128)(2,1)S(1)}, bf16[4,1,4,24,3840]{4,3,2,1,0:T(8,128)(2,1)}, u32[]{:S(2)}, u32[]{:S(2)}) collective-permute-start(bf16[4,1,4,24,3840]{4,3,2,1,0:T(8,128)(2,1)S(1)} %constant_dynamic-update-slice_fusion.12), channel_id=1, source_target_pairs={{0,4},{4,0},{8,12},{12,8},{16,20},{20,16},{24,28},{28,24},{1,5},{5... | collective-permute-start | bytes 8847368 | tf_op jit(solution)/shard_map/ppermute | solution.py:254
  339.0 146.9 %collective-permute-start.60 = (bf16[4,1,4,96,768]{4,3,2,1,0:T(8,128)(2,1)}, bf16[4,1,4,96,768]{4,3,2,1,0:T(8,128)(2,1)}, u32[]{:S(2)}, u32[]{:S(2)}) collective-permute-start(bf16[4,1,4,96,768]{4,3,2,1,0:T(8,128)(2,1)} %constant_dynamic-slice_fusion.1), channel_id=1, source_target_pairs={{0,4},{4,0},{8,12},{12,8},{16,20},{20,16},{24,28},{28,24},{1,5},{5... | collective-permute-start | bytes 7077896 | tf_op jit(solution)/shard_map/ppermute | solution.py:254
  341.1 150.3 %collective-permute-start.53 = (bf16[4,1,4,24,3072]{4,3,2,1,0:T(8,128)(2,1)}, bf16[4,1,4,24,3072]{4,3,2,1,0:T(8,128)(2,1)}, u32[]{:S(2)}, u32[]{:S(2)}) collective-permute-start(bf16[4,1,4,24,3072]{4,3,2,1,0:T(8,128)(2,1)} %constant_dynamic-slice_fusion.8), channel_id=1, source_target_pairs={{0,4},{4,0},{8,12},{12,8},{16,20},{20,16},{24,28},{28,24},{1,5},{5... | collective-permute-start | bytes 7077896 | tf_op jit(solution)/shard_map/ppermute | solution.py:254
  341.8 75.7 %collective-permute-start.43 = (bf16[2,128,256]{2,1,0:T(8,128)(2,1)}, bf16[2,128,256]{2,1,0:T(8,128)(2,1)}, u32[]{:S(2)}, u32[]{:S(2)}) collective-permute-start(bf16[2,128,256]{2,1,0:T(8,128)(2,1)} %get-tuple-element.115), channel_id=1, source_target_pairs={{0,1},{1,0},{2,3},{3,2},{4,5},{5,4},{6,7},{7,6},{8,9},{9,8},{10,11... | collective-permute-start | bytes 393224 | tf_op jit(solution)/shard_map/ppermute | solution.py:254
  343.6 76.3 %collective-permute-start.44 = (bf16[2,128,256]{2,1,0:T(8,128)(2,1)}, bf16[2,128,256]{2,1,0:T(8,128)(2,1)}, u32[]{:S(2)}, u32[]{:S(2)}) collective-permute-start(bf16[2,128,256]{2,1,0:T(8,128)(2,1)} %get-tuple-element.114), channel_id=1, source_target_pairs={{0,2},{1,3},{2,0},{3,1},{4,6},{5,7},{6,4},{7,5},{8,10},{9,11},{10,... | collective-permute-start | bytes 393224 | tf_op jit(solution)/shard_map/ppermute | solution.py:254
  344.1 78.7 %collective-permute-start.45 = (bf16[2,128,256]{2,1,0:T(8,128)(2,1)}, bf16[2,128,256]{2,1,0:T(8,128)(2,1)}, u32[]{:S(2)}, u32[]{:S(2)}) collective-permute-start(bf16[2,128,256]{2,1,0:T(8,128)(2,1)} %get-tuple-element.113), channel_id=1, source_target_pairs={{0,3},{1,2},{2,1},{3,0},{4,7},{5,6},{6,5},{7,4},{8,11},{9,10},{10,... | collective-permute-start | bytes 393224 | tf_op jit(solution)/shard_map/ppermute | solution.py:254
  417.5 31.3 %collective-permute-start.40 = (bf16[2,128,768]{2,1,0:T(8,128)(2,1)}, bf16[2,128,768]{2,1,0:T(8,128)(2,1)}, u32[]{:S(2)}, u32[]{:S(2)}) collective-permute-start(bf16[2,128,768]{2,1,0:T(8,128)(2,1)} %get-tuple-element.94), channel_id=1, source_target_pairs={{0,1},{1,0},{2,3},{3,2},{4,5},{5,4},{6,7},{7,6},{8,9},{9,8},{10,11... | collective-permute-start | bytes 1179656 | tf_op jit(solution)/shard_map/ppermute | solution.py:254
  419.9 30.8 %collective-permute-start.41 = (bf16[2,128,768]{2,1,0:T(8,128)(2,1)}, bf16[2,128,768]{2,1,0:T(8,128)(2,1)}, u32[]{:S(2)}, u32[]{:S(2)}) collective-permute-start(bf16[2,128,768]{2,1,0:T(8,128)(2,1)} %get-tuple-element.93), channel_id=1, source_target_pairs={{0,2},{1,3},{2,0},{3,1},{4,6},{5,7},{6,4},{7,5},{8,10},{9,11},{10,... | collective-permute-start | bytes 1179656 | tf_op jit(solution)/shard_map/ppermute | solution.py:254
  422.8 30.4 %collective-permute-start.42 = (bf16[2,128,768]{2,1,0:T(8,128)(2,1)}, bf16[2,128,768]{2,1,0:T(8,128)(2,1)}, u32[]{:S(2)}, u32[]{:S(2)}) collective-permute-start(bf16[2,128,768]{2,1,0:T(8,128)(2,1)} %get-tuple-element.92), channel_id=1, source_target_pairs={{0,3},{1,2},{2,1},{3,0},{4,7},{5,6},{6,5},{7,4},{8,11},{9,10},{10,... | collective-permute-start | bytes 1179656 | tf_op jit(solution)/shard_map/ppermute | solution.py:254
  450.7 32.9 %collective-permute-start.32 = (bf16[2,128,768]{2,1,0:T(8,128)(2,1)S(1)}, bf16[2,128,768]{2,1,0:T(8,128)(2,1)S(1)}, u32[]{:S(2)}, u32[]{:S(2)}) collective-permute-start(bf16[2,128,768]{2,1,0:T(8,128)(2,1)S(1)} %copy-done.40), channel_id=1, source_target_pairs={{0,2},{1,3},{2,0},{3,1},{4,6},{5,7},{6,4},{7,5},{8,10},{9,11},{10,... | collective-permute-start | bytes 1179656 | tf_op jit(solution)/shard_map/ppermute | solution.py:254
  453.2 30.4 %collective-permute-start.33 = (bf16[2,128,768]{2,1,0:T(8,128)(2,1)S(1)}, bf16[2,128,768]{2,1,0:T(8,128)(2,1)S(1)}, u32[]{:S(2)}, u32[]{:S(2)}) collective-permute-start(bf16[2,128,768]{2,1,0:T(8,128)(2,1)S(1)} %copy-done.39), channel_id=1, source_target_pairs={{0,3},{1,2},{2,1},{3,0},{4,7},{5,6},{6,5},{7,4},{8,11},{9,10},{10,... | collective-permute-start | bytes 1179656 | tf_op jit(solution)/shard_map/ppermute | solution.py:254
  461.1 35.1 %collective-permute-start.46 = (bf16[4,1,4,24,3584]{4,3,2,1,0:T(8,128)(2,1)S(1)}, bf16[4,1,4,24,3584]{4,3,2,1,0:T(8,128)(2,1)S(1)}, u32[]{:S(2)}, u32[]{:S(2)}) collective-permute-start(bf16[4,1,4,24,3584]{4,3,2,1,0:T(8,128)(2,1)S(1)} %constant_dynamic-slice_fusion.15), channel_id=1, source_target_pairs={{0,4},{4,0},{8,12},{12,8},{16,20},{20,16},{24,28},{28,24},{1,5},{5... | collective-permute-start | bytes 8257544 | tf_op jit(solution)/shard_map/ppermute | solution.py:254
  489.2 53.0 %collective-permute-start.61 = (bf16[1,1,4,96,768]{4,3,2,1,0:T(8,128)(2,1)S(1)}, bf16[1,1,4,96,768]{4,3,2,1,0:T(8,128)(2,1)S(1)}, u32[]{:S(2)}, u32[]{:S(2)}) collective-permute-start(bf16[1,1,4,96,768]{4,3,2,1,0:T(8,128)(2,1)S(1)} %get-tuple-element.85), channel_id=1, source_target_pairs={{0,8},{4,12},{8,0},{12,4},{16,24},{20,28},{24,16},{28,20},{1,9},{5... | collective-permute-start | bytes 1769480 | tf_op jit(solution)/shard_map/ppermute | solution.py:254
  489.9 63.0 %collective-permute-start.62 = (bf16[1,1,4,96,768]{4,3,2,1,0:T(8,128)(2,1)S(1)}, bf16[1,1,4,96,768]{4,3,2,1,0:T(8,128)(2,1)S(1)}, u32[]{:S(2)}, u32[]{:S(2)}) collective-permute-start(bf16[1,1,4,96,768]{4,3,2,1,0:T(8,128)(2,1)S(1)} %get-tuple-element.87), channel_id=1, source_target_pairs={{0,16},{4,20},{8,24},{12,28},{16,0},{20,4},{24,8},{28,12},{1,17},{... | collective-permute-start | bytes 1769480 | tf_op jit(solution)/shard_map/ppermute | solution.py:254
  494.1 24.1 %collective-permute-start.54 = (bf16[1,1,4,24,3072]{4,3,2,1,0:T(8,128)(2,1)S(1)}, bf16[1,1,4,24,3072]{4,3,2,1,0:T(8,128)(2,1)S(1)}, u32[]{:S(2)}, u32[]{:S(2)}) collective-permute-start(bf16[1,1,4,24,3072]{4,3,2,1,0:T(8,128)(2,1)S(1)} %get-tuple-element.88), channel_id=1, source_target_pairs={{0,8},{4,12},{8,0},{12,4},{16,24},{20,28},{24,16},{28,20},{1,9},{5... | collective-permute-start | bytes 1769480 | tf_op jit(solution)/shard_map/ppermute | solution.py:254
  495.7 38.9 %collective-permute-start.55 = (bf16[1,1,4,24,3072]{4,3,2,1,0:T(8,128)(2,1)S(1)}, bf16[1,1,4,24,3072]{4,3,2,1,0:T(8,128)(2,1)S(1)}, u32[]{:S(2)}, u32[]{:S(2)}) collective-permute-start(bf16[1,1,4,24,3072]{4,3,2,1,0:T(8,128)(2,1)S(1)} %get-tuple-element.90), channel_id=1, source_target_pairs={{0,16},{4,20},{8,24},{12,28},{16,0},{20,4},{24,8},{28,12},{1,17},{... | collective-permute-start | bytes 1769480 | tf_op jit(solution)/shard_map/ppermute | solution.py:254
  496.2 42.7 %collective-permute-start.56 = (bf16[1,1,4,24,3072]{4,3,2,1,0:T(8,128)(2,1)S(1)}, bf16[1,1,4,24,3072]{4,3,2,1,0:T(8,128)(2,1)S(1)}, u32[]{:S(2)}, u32[]{:S(2)}) collective-permute-start(bf16[1,1,4,24,3072]{4,3,2,1,0:T(8,128)(2,1)S(1)} %get-tuple-element.89), channel_id=1, source_target_pairs={{0,24},{4,28},{8,16},{12,20},{16,8},{20,12},{24,0},{28,4},{1,25},{... | collective-permute-start | bytes 1769480 | tf_op jit(solution)/shard_map/ppermute | solution.py:254
  518.2 35.2 %collective-permute-start.63 = (bf16[1,1,4,96,768]{4,3,2,1,0:T(8,128)(2,1)S(1)}, bf16[1,1,4,96,768]{4,3,2,1,0:T(8,128)(2,1)S(1)}, u32[]{:S(2)}, u32[]{:S(2)}) collective-permute-start(bf16[1,1,4,96,768]{4,3,2,1,0:T(8,128)(2,1)S(1)} %get-tuple-element.86), channel_id=1, source_target_pairs={{0,24},{4,28},{8,16},{12,20},{16,8},{20,12},{24,0},{28,4},{1,25},{... | collective-permute-start | bytes 1769480 | tf_op jit(solution)/shard_map/ppermute | solution.py:254
  534.6 33.6 %collective-permute-start.47 = (bf16[1,1,4,24,3584]{4,3,2,1,0:T(8,128)(2,1)S(1)}, bf16[1,1,4,24,3584]{4,3,2,1,0:T(8,128)(2,1)S(1)}, u32[]{:S(2)}, u32[]{:S(2)}) collective-permute-start(bf16[1,1,4,24,3584]{4,3,2,1,0:T(8,128)(2,1)S(1)} %get-tuple-element.82), channel_id=1, source_target_pairs={{0,8},{4,12},{8,0},{12,4},{16,24},{20,28},{24,16},{28,20},{1,9},{5... | collective-permute-start | bytes 2064392 | tf_op jit(solution)/shard_map/ppermute | solution.py:254
  538.8 31.3 %collective-permute-start.48 = (bf16[1,1,4,24,3584]{4,3,2,1,0:T(8,128)(2,1)S(1)}, bf16[1,1,4,24,3584]{4,3,2,1,0:T(8,128)(2,1)S(1)}, u32[]{:S(2)}, u32[]{:S(2)}) collective-permute-start(bf16[1,1,4,24,3584]{4,3,2,1,0:T(8,128)(2,1)S(1)} %get-tuple-element.84), channel_id=1, source_target_pairs={{0,16},{4,20},{8,24},{12,28},{16,0},{20,4},{24,8},{28,12},{1,17},{... | collective-permute-start | bytes 2064392 | tf_op jit(solution)/shard_map/ppermute | solution.py:254
  563.6 16.1 %collective-permute-start.64 = (bf16[1,1,1,96,768]{4,3,2,1,0:T(8,128)(2,1)S(1)}, bf16[1,1,1,96,768]{4,3,2,1,0:T(8,128)(2,1)S(1)}, u32[]{:S(2)}, u32[]{:S(2)}) collective-permute-start(bf16[1,1,1,96,768]{4,3,2,1,0:T(8,128)(2,1)S(1)} %get-tuple-element.107), channel_id=1, source_target_pairs={{0,1},{1,0},{2,3},{3,2},{4,5},{5,4},{6,7},{7,6},{8,9},{9,8},{10,11... | collective-permute-start | bytes 442376 | tf_op jit(solution)/shard_map/ppermute | solution.py:254
  563.6 18.0 %collective-permute-start.65 = (bf16[1,1,1,96,768]{4,3,2,1,0:T(8,128)(2,1)S(1)}, bf16[1,1,1,96,768]{4,3,2,1,0:T(8,128)(2,1)S(1)}, u32[]{:S(2)}, u32[]{:S(2)}) collective-permute-start(bf16[1,1,1,96,768]{4,3,2,1,0:T(8,128)(2,1)S(1)} %get-tuple-element.109), channel_id=1, source_target_pairs={{0,2},{1,3},{2,0},{3,1},{4,6},{5,7},{6,4},{7,5},{8,10},{9,11},{10,... | collective-permute-start | bytes 442376 | tf_op jit(solution)/shard_map/ppermute | solution.py:254
  570.5 15.3 %collective-permute-start.50 = (bf16[1,1,1,24,3584]{4,3,2,1,0:T(8,128)(2,1)S(1)}, bf16[1,1,1,24,3584]{4,3,2,1,0:T(8,128)(2,1)S(1)}, u32[]{:S(2)}, u32[]{:S(2)}) collective-permute-start(bf16[1,1,1,24,3584]{4,3,2,1,0:T(8,128)(2,1)S(1)} %get-tuple-element.104), channel_id=1, source_target_pairs={{0,1},{1,0},{2,3},{3,2},{4,5},{5,4},{6,7},{7,6},{8,9},{9,8},{10,11... | collective-permute-start | bytes 516104 | tf_op jit(solution)/shard_map/ppermute | solution.py:254
  (111 other events, 1137.9 us)
